TPU v7x, 32 devices: a whole 2x2x4 slice. The times are simulated.
32 devices in a mesh: band: 8 (over z, y), tm: 4 (over x, core).
Axes of the slice: x: 2, y: 2, z: 4, core: 2. Of those that a mesh axis runs over, the one named last changes fastest.
Arguments:
- fields: bfloat16 [512, 704, 1440], P('tm', 'band'), may hold values from -6 to 6
- wave_table: int32 [384], replicated, may hold values from 0 to 383, as said below
- day_of_year: int32 [512], P('tm'), may hold values from 0 to 364, as said below
- ar_coef: float32 [384, 384], P('band'), may hold values from -0.9 to 0.9
- log_var: float32 [384, 384], P('band'), may hold values from 0 to 2.5
Outputs:
- innovation: bfloat16 [512, 2, 384, 384], P('tm', None, 'band')
- grad_coef: float32 [384, 384], P('band', 'tm')
- grad_var: float32 [384, 384], P('band', 'tm')
Inputs may be any that keep to these rules, and one draw needn't show every extreme that they name: `wave_table`: every wavenumber below 384 appears once; slots 2 k and 2 k + 1 hold some m and 383 - m. `day_of_year`: consecutive days follow one another in the year, 364 being followed by 0; both 364 and 0 occur.
All inputs are finite; a program needn't handle non-finite values.
Results may differ from a plain program's by a relative error of at most 0.008.
Values may be sent and summed in bfloat16 or wider, within the bound.
No kernel may reach another device: no remote copies, remote signals or barrier semaphores. Data moves between devices by JAX's collectives and lax.ppermute only.
A program may use at most 256 MiB of HBM per device.

v0:
```python
import math

import jax
import jax.numpy as jnp
from jax import lax
from jax.sharding import PartitionSpec as P


def shifted(block, axis, distance):
    devices = range(lax.axis_size(axis))
    route = [(i - distance, i) for i in devices if i - distance in devices]
    return lax.ppermute(block, axis, route)


def fourier_table(wave_list, lon_count):
    lon_index = jnp.arange(lon_count, dtype=jnp.int32)
    phase_index = lon_index[:, None] * wave_list[None, :] % lon_count
    angle_rad = phase_index.astype(jnp.float32) * (2.0 * math.pi / lon_count)
    return jnp.concatenate([jnp.cos(angle_rad), -jnp.sin(angle_rad)], axis=1).astype(jnp.bfloat16)


def legendre_setup(wave_list, lat_count):
    colatitude = (jnp.arange(lat_count, dtype=jnp.float32) + 0.5) * (math.pi / lat_count)
    cosines = jnp.cos(colatitude)
    sine_vals = jnp.sin(colatitude)
    wave_order = wave_list.astype(jnp.float32)[:, None]
    log_start = 0.5 * (
        jnp.log(wave_order + 0.5)
        + jax.scipy.special.gammaln(wave_order + 0.5)
        - jax.scipy.special.gammaln(wave_order + 1.0)
        - 0.5 * math.log(math.pi)
    )
    log_start = log_start + wave_order * jnp.log(sine_vals)[None, :]
    weights = sine_vals * (math.pi / lat_count)
    return (wave_order, cosines, log_start, weights)


def legendre_step(degree_index, carry_state, wave_order, cosines, log_start):
    lagged, current, log_scale = carry_state
    degree_f = jnp.asarray(degree_index).astype(jnp.float32)
    above = degree_f - wave_order
    denominator = jnp.maximum(above * (degree_f + wave_order), 1.0)
    first_coef = jnp.sqrt(jnp.maximum((4.0 * degree_f * degree_f - 1.0) / denominator, 0.0))
    second_coef = jnp.sqrt(
        jnp.maximum(
            ((degree_f - 1.0) ** 2 - wave_order * wave_order)
            * (2.0 * degree_f + 1.0)
            / ((2.0 * degree_f - 3.0) * denominator),
            0.0,
        )
    )
    advanced = first_coef * cosines[None, :] * current - second_coef * lagged
    moving = above > 0.5
    at_start = jnp.abs(above) < 0.5
    new_lagged = jnp.where(moving, current, 0.0)
    new_current = jnp.where(moving, advanced, jnp.where(at_start, 1.0, 0.0))
    new_scale = jnp.where(at_start, log_start, log_scale)
    largest = jnp.maximum(jnp.abs(new_current), 1.0)
    new_lagged = new_lagged / largest
    new_current = new_current / largest
    new_scale = new_scale + jnp.log(largest)
    value = jnp.where(above > -0.5, new_current * jnp.exp(new_scale), 0.0)
    return ((new_lagged, new_current, new_scale), value)


def legendre_rows(wave_list, lat_count, degree_count):
    wave_order, cosines, log_start, weights = legendre_setup(wave_list, lat_count)
    zero_state = jnp.zeros((wave_list.shape[0], lat_count), jnp.float32)
    empty_rows = jnp.zeros((degree_count, wave_list.shape[0], lat_count), jnp.bfloat16)

    def run_block(block_index, carry_pair):
        carry_state, legendre = carry_pair
        pieces = []
        for step_index in range(16):
            carry_state, value = legendre_step(
                block_index * 16 + step_index, carry_state, wave_order, cosines, log_start
            )
            pieces.append((value * weights[None, :]).astype(jnp.bfloat16))
        legendre = lax.dynamic_update_slice_in_dim(legendre, jnp.stack(pieces), block_index * 16, 0)
        return (carry_state, legendre)

    final_state, legendre = lax.fori_loop(
        0, degree_count // 16, run_block, ((zero_state, zero_state, zero_state), empty_rows)
    )
    return legendre


def per_device(fields, wave_table, day_of_year, ar_coef, log_var):
    band_count = lax.axis_size("band")
    time_count = lax.axis_size("tm")
    slot_count = ar_coef.shape[0]
    degree_count = ar_coef.shape[1]
    day_count = fields.shape[0]
    lat_local = fields.shape[1]
    lat_count = lat_local * band_count
    total_days = day_count * time_count
    dft_table = fourier_table(wave_table, fields.shape[2])
    coeffs = jnp.einsum("djk,kq->dqj", fields, dft_table, preferred_element_type=jnp.float32)
    coeffs = coeffs.astype(jnp.bfloat16).reshape(day_count, 2, wave_table.shape[0], lat_local)
    own_waves = lax.dynamic_slice_in_dim(
        wave_table, lax.axis_index("band") * slot_count, slot_count
    )
    legendre = legendre_rows(own_waves, lat_count, degree_count)
    gathered = lax.all_to_all(coeffs, "band", split_axis=2, concat_axis=3, tiled=True)
    spectral = jnp.einsum("dcsj,lsj->dcsl", gathered, legendre, preferred_element_type=jnp.float32)
    carried = shifted(spectral[-1].astype(jnp.bfloat16), "tm", 1).astype(jnp.float32)
    previous = jnp.concatenate([carried[None], spectral[:-1]], axis=0)
    degree_list = jnp.arange(degree_count, dtype=jnp.int32)
    valid_mask = (degree_list[None, :] >= own_waves[:, None]).astype(jnp.float32)
    season = 1.0 + 0.5 * jnp.cos(day_of_year.astype(jnp.float32) * (2.0 * math.pi / 365.0))
    inverse_var = jnp.exp(-log_var)[None, :, :] / season[:, None, None]
    residual = spectral - ar_coef[None, None, :, :] * previous
    innovation = (residual * jnp.sqrt(inverse_var)[:, None] * valid_mask).astype(jnp.bfloat16)
    partial_coef = jnp.sum(residual * previous * inverse_var[:, None], axis=(0, 1))
    partial_var = jnp.sum(0.5 * (1.0 - residual * residual * inverse_var[:, None]), axis=(0, 1))
    summed_coef, summed_var = (
        lax.psum_scatter(
            partial_coef.astype(jnp.bfloat16), "tm", scatter_dimension=1, tiled=True
        ).astype(jnp.float32),
        lax.psum_scatter(
            partial_var.astype(jnp.bfloat16), "tm", scatter_dimension=1, tiled=True
        ).astype(jnp.float32),
    )
    column_width = degree_count // time_count
    local_mask = lax.dynamic_slice_in_dim(
        valid_mask, lax.axis_index("tm") * column_width, column_width, 1
    )
    grad_coef = -local_mask * summed_coef / (2.0 * total_days)
    grad_var = local_mask * summed_var / (2.0 * total_days)
    return (innovation, grad_coef, grad_var)


def solution(mesh):
    in_specs = (P("tm", "band", None), P(), P("tm"), P("band", None), P("band", None))
    out_specs = (P("tm", None, "band", None), P("band", "tm"), P("band", "tm"))
    return jax.shard_map(
        per_device, mesh=mesh, in_specs=in_specs, out_specs=out_specs, check_vma=False
    )
```

profile of v0, /device:TPU:0, one launch (start us, length us, event | category | flops | bytes accessed | tf_op | source)
XLA Modules:
  0.0 596.5 jit_solution(16164508650489267742)
XLA Ops:
  7.2 10.3 %cosine_convert_fusion = (bf16[1440,384]{1,0:T(8,128)(2,1)S(1)}, bf16[1440,384]{1,0:T(8,128)(2,1)S(1)}) fusion(s32[384]{0:T(512)} %param.8), kind=kLoop, calls=%fused_computation.301 | loop fusion | flops 6635520 | bytes 2213376 | tf_op jit(solution)/shard_map/convert.2
  17.4 33.4 %convolution_convert_fusion = bf16[768,128,88]{1,0,2:T(8,128)(2,1)} fusion(bf16[128,88,1440]{0,2,1:T(8,128)(2,1)} %param.7, bf16[1440,384]{1,0:T(8,128)(2,1)S(1)} %get-tuple-element.715, bf16[1440,384]{1,0:T(8,128)(2,1)S(1)} %get-tuple-element.714), kind=kOutput, calls=%fused_computation.290 | convolution fusion | flops 24927240192 | bytes 51953664 | tf_op jit(solution)/shard_map/djk,kq->dqj/dot_general | solution.py:98
  50.9 32.1 %copy.12 = bf16[128,2,384,88]{0,1,3,2:T(2,128)(2,1)} copy(bf16[128,2,384,88]{0,2,1,3:T(8,128)(2,1)} %bitcast.318) | data formatting | bytes 34603008 | tf_op jit(solution)/shard_map/reshape | solution.py:99
  83.0 7.3 %all-to-all-start = ((bf16[128,2,384,88]{0,1,3,2:T(2,128)(2,1)}), bf16[128,2,384,88]{0,1,3,2:T(2,128)(2,1)}, u32[]{:S(2)}, u32[]{:S(2)}) async-start(bf16[128,2,384,88]{0,1,3,2:T(2,128)(2,1)} %copy.12), calls=%async_computation | async-start | bytes 34603008 | tf_op jit(solution)/shard_map/all_to_all | solution.py:104
  90.4 0.8 add_multiply_fusion.1
  91.3 9.7 %broadcast_in_dim.1481 = bf16[384,48,704]{2,1,0:T(8,128)(2,1)} broadcast(bf16[]{:T(256)} %constant.373.clone.1), dimensions={} | broadcast | bytes 25952258 | tf_op jit(solution)/shard_map/broadcast_in_dim | solution.py:69
  101.0 133.2 %while.24 = (s32[]{:T(128)}, f32[48,704]{1,0:T(8,128)S(1)}, f32[48,704]{1,0:T(8,128)S(1)}, f32[48,704]{1,0:T(8,128)S(1)}, bf16[384,48,704]{2,1,0:T(8,128)(2,1)},...) while((s32[]{:T(128)}, f32[48,704]{1,0:T(8,128)S(1)}, ...), condition=%wide.region_1.2_spmd.clone.clone, body=%wide.region_0.1_spmd.clone.clone.sunk | while | flops 13569573 | bytes 14862858 | solution.py:82
  104.0 0.3 fusion.152
  105.3 1.1 constant_dynamic-update-slice_fusion.2
  109.5 0.3 fusion.152
  110.8 1.1 constant_dynamic-update-slice_fusion.2
  115.1 0.3 fusion.152
  116.3 1.1 constant_dynamic-update-slice_fusion.2
  121.9 1.1 constant_dynamic-update-slice_fusion.2
  126.1 0.3 fusion.152
  127.4 1.1 constant_dynamic-update-slice_fusion.2
  131.7 0.3 fusion.152
  133.0 1.1 constant_dynamic-update-slice_fusion.2
  137.3 0.3 fusion.152
  138.5 1.2 constant_dynamic-update-slice_fusion.2
  142.9 0.3 fusion.152
  144.1 1.2 constant_dynamic-update-slice_fusion.2
  149.7 1.1 constant_dynamic-update-slice_fusion.2
  155.3 1.1 constant_dynamic-update-slice_fusion.2
  159.5 0.3 fusion.152
  160.8 1.2 constant_dynamic-update-slice_fusion.2
  165.1 0.3 fusion.152
  166.4 1.1 constant_dynamic-update-slice_fusion.2
  170.7 0.3 fusion.152
  171.9 1.1 constant_dynamic-update-slice_fusion.2
  176.2 0.3 fusion.152
  177.5 1.1 constant_dynamic-update-slice_fusion.2
  181.8 0.3 fusion.152
  183.0 1.1 constant_dynamic-update-slice_fusion.2
  188.6 1.1 constant_dynamic-update-slice_fusion.2
  192.8 0.3 fusion.152
  194.1 1.1 constant_dynamic-update-slice_fusion.2
  198.4 0.3 fusion.152
  199.7 1.1 constant_dynamic-update-slice_fusion.2
  205.2 1.1 constant_dynamic-update-slice_fusion.2
  209.5 0.3 fusion.152
  210.7 1.1 constant_dynamic-update-slice_fusion.2
  215.0 0.3 fusion.152
  216.3 1.1 constant_dynamic-update-slice_fusion.2
  220.6 0.3 fusion.152
  221.9 1.2 constant_dynamic-update-slice_fusion.2
  227.5 1.1 constant_dynamic-update-slice_fusion.2
  233.0 1.1 constant_dynamic-update-slice_fusion.2
  234.3 9.5 %broadcast_divide_fusion = (f32[128,48,384]{2,0,1:T(8,128)}, f32[128,48,384]{2,0,1:T(8,128)}) fusion(f32[128]{0:T(128)S(1)} %multiply_add_fusion.1, f32[48,384]{1,0:T(8,128)S(1)} %negate_exponential_fusion), kind=kLoop, calls=%fused_computation.292 | loop fusion | flops 2359296 | bytes 18948608 | tf_op jit(solution)/shard_map/div | solution.py:111
  243.9 220.6 %all-to-all-done = bf16[128,2,384,88]{0,1,3,2:T(2,128)(2,1)} async-done(((bf16[128,2,384,88]{0,1,3,2:T(2,128)(2,1)}), bf16[128,2,384,88]{0,1,3,2:T(2,128)(2,1)}, u32[]{:S(2)}, u32[]{:S(2)}) %all-to-all-start) | async-done | bytes 17301536 | tf_op jit(solution)/shard_map/all_to_all | solution.py:104
  464.5 15.6 %copy.13 = bf16[128,2,8,48,88]{0,4,2,1,3:T(8,128)(2,1)} copy(bf16[128,2,8,48,88]{0,1,4,3,2:T(2,128)(2,1)} %bitcast.6) | data formatting | bytes 34603008 | tf_op jit(solution)/shard_map/all_to_all | solution.py:104
  480.1 34.1 %fusion.91 = f32[128,2,48,384]{3,0,1,2:T(8,128)} fusion(bf16[128,2,48,704]{0,3,1,2:T(8,128)(2,1)} %bitcast.317, bf16[384,48,704,1]{2,1,0,3:T(8,128)(2,1)} %bitcast.316), kind=kOutput, calls=%fused_computation.291 | convolution fusion | flops 6643777536 | bytes 62128128 | tf_op jit(solution)/shard_map/dcsj,lsj->dcsl/dot_general | solution.py:105
  514.2 1.4 slice.9
  515.6 1.3 collective-permute-start
  517.0 0.8 collective-permute-done
  517.9 25.1 %multiply_reduce_fusion = (bf16[48,384]{1,0:T(8,128)(2,1)S(1)}, bf16[48,384]{1,0:T(8,128)(2,1)S(1)}, bf16[128,2,48,384]{3,0,1,2:T(8,128)(2,1)}) fusion(f32[128,48,384]{2,0,1:T(8,128)} %get-tuple-element.710, f32[128,2,48,384]{3,0,1,2:T(8,128)} %fusion.91, f32[127,2,48,384]{3,0,1,2:T(8,128)} %bitcast.315, f32[1,2,48,384]{3,0,1,2:T(1,128)S(1)} %reshape.1563, ...), kind=kLoop, calls=%fused_computation.286 | loop fusion | flops 66023424 | bytes 66281472 | tf_op jit(solution)/shard_map/reduce_sum | solution.py:115
  543.0 0.7 copy.20
  543.9 0.7 copy.22
  544.6 13.0 %copy.16 = bf16[128,2,48,384]{3,2,1,0:T(8,128)(2,1)} copy(bf16[128,2,48,384]{3,0,1,2:T(8,128)(2,1)} %get-tuple-element.709) | data formatting | bytes 18874368
  557.6 8.5 %reduce-scatter.7.cloned.1.call-done = bf16[96,48]{1,0:T(8,128)(2,1)} async-done(((bf16[384,48]{1,0:T(8,128)(2,1)}), bf16[96,48]{1,0:T(8,128)(2,1)}) %reduce-scatter.7.cloned.1.call-update) | async-done | bytes 9232
  566.1 0.8 copy.21
  566.9 21.2 %reduce-scatter.9.cloned.1.call-done = bf16[96,48]{1,0:T(8,128)(2,1)} async-done(((bf16[384,48]{1,0:T(8,128)(2,1)}), bf16[96,48]{1,0:T(8,128)(2,1)}) %reduce-scatter.9.cloned.1.call-update) | async-done | bytes 9232
  588.1 0.8 copy.23
  589.0 0.7 multiply_multiply_fusion
  (628 shorter events, 92.1 us)
Async XLA Ops:
  83.0 381.5 %all-to-all-start = ((bf16[128,2,384,88]{0,1,3,2:T(2,128)(2,1)}), bf16[128,2,384,88]{0,1,3,2:T(2,128)(2,1)}, u32[]{:S(2)}, u32[]{:S(2)}) async-start(bf16[128,2,384,88]{0,1,3,2:T(2,128)(2,1)} %copy.12), calls=%async_computation | async-start | bytes 34603008 | tf_op jit(solution)/shard_map/all_to_all | solution.py:104
  90.3 475.8 %reduce-scatter.7.cloned.1.call-start = ((), (), s32[]{:S(2)}) async-start(), calls=%async_computation.3 | async-start | bytes 122880
  101.0 133.3 %copy-start.2 = (s32[128]{0:T(128)S(1)}, s32[128]{0:T(128)}, u32[]{:S(2)}) copy-start(s32[128]{0:T(128)} %param.9) | copy-start | bytes 1540
  101.0 133.3 %copy-start.1 = (f32[48,384]{1,0:T(8,128)S(1)}, f32[48,384]{1,0:T(8,128)}, u32[]{:S(2)}) copy-start(f32[48,384]{1,0:T(8,128)} %param.11) | copy-start | bytes 221188
  480.1 37.9 %copy-start = (f32[48,384]{1,0:T(8,128)S(1)}, f32[48,384]{1,0:T(8,128)}, u32[]{:S(2)}) copy-start(f32[48,384]{1,0:T(8,128)} %param.10) | copy-start | bytes 221188
  515.6 2.2 collective-permute-start
  543.8 44.3 %reduce-scatter.9.cloned.1.call-start = ((), (), s32[]{:S(2)}) async-start(), calls=%async_computation.4 | async-start | bytes 122880
Sparse Core Ops, SparseCore 0:
  543.9 22.1 reduce-scatter.6
  568.6 19.5 reduce-scatter.8
where the time goes:
time: 597 us
  waiting for transfers between devices  251 us (42%)
  other arithmetic  143 us (24%)
  local copies, waits for them, and re-layouts  102 us (17%)
  matrix products  67.5 us (11%)
  between operations  14.2 us (2%)
  loops' own time  10.5 us (2%)
  starting transfers between devices  8.66 us (1%)
    all_to_all x1, waiting for transfers between devices, per_device(): lax.all_to_all(coeffs, 'band', split_axis=2, concat_axis=3, tiled=True)  221 us
    while x360, other arithmetic  80.3 us
    dot_general x1, matrix products, per_device(): jnp.einsum('dcsj,lsj->dcsl', gathered, legendre, preferred_element_type=j...  34.1 us
    dot_general x1, matrix products, per_device(): jnp.einsum('djk,kq->dqj', fields, dft_table, preferred_element_type=jnp.f...  33.4 us
    reshape x1, local copies, waits for them, and re-layouts, per_device(): coeffs.astype(jnp.bfloat16)  32.1 us
    unnamed x4, waiting for transfers between devices  29.7 us
    dynamic_update_slice x24, local copies, waits for them, and re-layouts, run_block(): lax.dynamic_update_slice_in_dim(legendre, jnp.stack(pieces), block_index...  26.9 us
    reduce_sum x1, other arithmetic, per_device(): jnp.sum(0.5 * (1.0 - residual * residual * inverse_var[:, None]), axis=(0...  25.1 us
  transfers between devices with their start and end apart: 4, of which 4 were waited for; matrix products, arithmetic and copies ran while one was open for 26% of the time, Pallas kernels for 0%

commit v1 on v0

v1 whole, which is shorter than its diff:
```python
import functools
import math

import jax
import jax.numpy as jnp
import numpy as np
from jax import lax
from jax.experimental import pallas as pl
from jax.experimental.pallas import tpu as pltpu
from jax.sharding import PartitionSpec as P

LANES = 128
TILE = 16
VMEM_LIMIT = 56 * 1024 * 1024


def round_up(value, unit):
    return -(-value // unit) * unit


def fourier_columns(waves, lon_count):
    fine_count = 32
    coarse_count = lon_count // fine_count
    scale = 2.0 * math.pi / lon_count

    def parts(lons):
        angle = (lons[:, None] * waves[None, :] % lon_count).astype(jnp.float32) * scale
        return jnp.cos(angle), jnp.sin(angle)

    coarse_cos, coarse_sin = parts(jnp.arange(coarse_count, dtype=jnp.int32) * fine_count)
    fine_cos, fine_sin = parts(jnp.arange(fine_count, dtype=jnp.int32))
    coarse_cos, coarse_sin = coarse_cos[:, None], coarse_sin[:, None]
    fine_cos, fine_sin = fine_cos[None], fine_sin[None]
    cosine = coarse_cos * fine_cos - coarse_sin * fine_sin
    minus_sine = -(coarse_sin * fine_cos + coarse_cos * fine_sin)
    shape = (lon_count, waves.shape[0])
    return cosine.reshape(shape), minus_sine.reshape(shape)


def table_kernel(steps, lane_tiles, top, low_ref, first_ref, second_ref, cos_ref, weight_ref, out_ref, rows_ref, scale_ref):
    tiles = range(lane_tiles)
    low = low_ref[...]
    high = top - low
    low_next = low + 1.0
    lat_count = out_ref.shape[2]

    def lanes(ref, tile):
        return ref[:, tile * LANES : (tile + 1) * LANES]

    cosines = [lanes(cos_ref, t) for t in tiles]
    weights = [lanes(weight_ref, t) for t in tiles]
    second = [lanes(second_ref, t) for t in tiles]
    for t in tiles:
        half = jnp.exp(0.5 * second[t])
        scale_ref[2, :, t * LANES : (t + 1) * LANES] = half * weights[t]
        scale_ref[3, :, t * LANES : (t + 1) * LANES] = half

    def block(index, carry):
        current, lagged, scale, last_inverse = carry
        for t in tiles:
            largest = jnp.maximum(jnp.maximum(jnp.abs(current[t]), jnp.abs(lagged[t])), 1.0)
            current[t] = current[t] / largest
            lagged[t] = lagged[t] / largest
            scale[t] = scale[t] + jnp.log(largest)
            half = jnp.exp(0.5 * scale[t])
            scale_ref[0, :, t * LANES : (t + 1) * LANES] = half * weights[t]
            scale_ref[1, :, t * LANES : (t + 1) * LANES] = half
        begin = (index * TILE).astype(jnp.float32)
        for step in range(TILE):
            row = begin + float(step)
            after = low < row
            above = row - jnp.where(after, low_next, 0.0)
            order = jnp.where(after, low, high)
            degree = above + order
            spread = above * (degree + order)
            square = 4.0 * degree * degree - 1.0
            root = lax.rsqrt(jnp.maximum(square * spread, 1.0))
            factor = square * root
            inverse = spread * root
            fresh = above == 0.0
            for t in tiles:
                advanced = factor * (cosines[t] * current[t] - last_inverse * lagged[t])
                lagged[t] = current[t]
                current[t] = jnp.where(fresh, 1.0, advanced)
                rows_ref[t, pl.ds(step, TILE, stride=TILE), :] = current[t]
            last_inverse = inverse
        renewed = (low_next >= begin) & (low_next < begin + float(TILE))
        for t in tiles:
            scale[t] = jnp.where(renewed, second[t], scale[t])
        row_index = lax.broadcasted_iota(jnp.int32, (TILE, LANES), 0).astype(jnp.float32) + begin
        for pair in range(TILE):
            mark = low[pair : pair + 1, :]
            before = (row_index <= mark) | (mark + 1.0 < begin)
            for t in tiles:
                span = slice(t * LANES, min((t + 1) * LANES, lat_count))
                width = span.stop - span.start
                here = slice(t * LANES, (t + 1) * LANES)
                values = rows_ref[t, pair * TILE : (pair + 1) * TILE, :]
                one = jnp.where(before, scale_ref[0, pair : pair + 1, here], scale_ref[2, pair : pair + 1, here])
                two = jnp.where(before, scale_ref[1, pair : pair + 1, here], scale_ref[3, pair : pair + 1, here])
                values = (values * one * two).astype(jnp.bfloat16)
                out_ref[pair, pl.ds(pl.multiple_of(index * TILE, TILE), TILE), span] = values[:, :width]
        return current, lagged, scale, last_inverse

    zeros = jnp.zeros((TILE, LANES), jnp.float32)
    start = (
        [zeros for _ in tiles],
        [zeros for _ in tiles],
        [lanes(first_ref, t) for t in tiles],
        zeros,
    )
    lax.fori_loop(0, steps // TILE, block, start)


def packed_table(low_waves, lat_begin, lat_half, lat_count, degree_count, steps):
    pair_count = low_waves.shape[0]
    lane_tiles = -(-lat_half // LANES)
    width = lane_tiles * LANES
    top = float(degree_count - 1)
    index = jnp.minimum(jnp.arange(width, dtype=jnp.int32), lat_half - 1) + lat_begin
    colatitude = (index.astype(jnp.float32) + 0.5) * (math.pi / lat_count)
    sines = jnp.sin(colatitude)
    log_sines = jnp.log(sines)
    low = low_waves.astype(jnp.float32)

    def log_start(order):
        base = 0.5 * (
            jnp.log(order + 0.5)
            + jax.scipy.special.gammaln(order + 0.5)
            - jax.scipy.special.gammaln(order + 1.0)
            - 0.5 * math.log(math.pi)
        )
        return base[:, None] + order[:, None] * log_sines[None, :]

    spread = lambda row: jnp.broadcast_to(row[None, :], (TILE, width))
    block = lambda *shape: pl.BlockSpec(shape, lambda i: (i,) + (0,) * (len(shape) - 1))
    whole = pl.BlockSpec((TILE, width), lambda i: (0, 0))
    return pl.pallas_call(
        functools.partial(table_kernel, steps, lane_tiles, top),
        grid=(pair_count // TILE,),
        in_specs=[block(TILE, LANES), block(TILE, width), block(TILE, width), whole, whole],
        out_specs=block(TILE, steps, lat_half),
        out_shape=jax.ShapeDtypeStruct((pair_count, steps, lat_half), jnp.bfloat16),
        scratch_shapes=[
            pltpu.VMEM((lane_tiles, TILE * TILE, LANES), jnp.float32),
            pltpu.VMEM((4, TILE, width), jnp.float32),
        ],
        compiler_params=pltpu.CompilerParams(vmem_limit_bytes=VMEM_LIMIT),
        cost_estimate=pl.CostEstimate(
            flops=pair_count * steps * width * 12, bytes_accessed=pair_count * steps * width * 2, transcendentals=0
        ),
    )(
        jnp.broadcast_to(low[:, None], (pair_count, LANES)),
        log_start(top - low),
        log_start(low),
        spread(jnp.cos(colatitude)),
        spread(sines * (math.pi / lat_count)),
    )


def gather_slots(in_ref, flat_ref, slot_ref):
    sources, lats, rows, days = in_ref.shape
    lat_half = sources * lats
    for part in range(2):
        for source in range(sources):
            values = in_ref[source, :, part * TILE : (part + 1) * TILE, :].astype(jnp.float32)
            flat_ref[pl.ds(source * lats * TILE, lats * TILE), :] = values.reshape(lats * TILE, days)
        for slot in range(TILE):
            column = flat_ref[pl.ds(slot, lat_half, stride=TILE), :]
            slot_ref[slot, :, part * days : (part + 1) * days] = column.astype(jnp.bfloat16)


def pair_sum(pair, low, table_ref, slot_ref):
    table = table_ref[pair]
    high_sum = jnp.dot(table, slot_ref[2 * pair], preferred_element_type=jnp.float32)
    low_sum = jnp.dot(table, slot_ref[2 * pair + 1], preferred_element_type=jnp.float32)
    row = lax.broadcasted_iota(jnp.int32, high_sum.shape, 0)
    return jnp.where(row <= low, high_sum, low_sum)


def partial_kernel(low_ref, in_ref, table_ref, out_ref, flat_ref, slot_ref):
    gather_slots(in_ref, flat_ref, slot_ref)

    def one(pair, carry):
        out_ref[pair] = pair_sum(pair, low_ref[pair], table_ref, slot_ref).astype(jnp.bfloat16)
        return carry

    lax.fori_loop(0, TILE // 2, one, 0)


def finish_kernel(
    low_ref, wave_ref, shift_ref, in_ref, table_ref, other_ref, ar_ref, half_ref, season_ref, *rest
):
    out_ref, misc_ref, flat_ref, slot_ref, turned_ref = rest[-5:]
    steps = table_ref.shape[1]
    days = out_ref.shape[0]
    degrees = out_ref.shape[3]
    lane_tiles = degrees // LANES
    gather_slots(in_ref, flat_ref, slot_ref)
    lane = lax.broadcasted_iota(jnp.int32, (steps, LANES), 1)
    turn = (
        lax.broadcasted_iota(jnp.int32, (days, days), 0) == lax.broadcasted_iota(jnp.int32, (days, days), 1)
    ).astype(jnp.bfloat16)
    pick_row = lax.broadcasted_iota(jnp.int32, (8, LANES), 0)
    pick_lane = lax.broadcasted_iota(jnp.int32, (8, LANES), 1)
    wanted = jnp.where(pick_row == 0, 0, jnp.where(pick_row == 1, 2, jnp.where(pick_row == 2, LANES - 1, pick_row - 0)))
    wanted = jnp.where(pick_row == 3, 1, jnp.where(pick_row == 4, 3, jnp.where(pick_row == 5, 4, wanted)))
    pick = ((pick_lane == wanted) & (pick_row < 6)).astype(jnp.bfloat16)
    transposed = (((1,), (1,)), ((), ()))

    def one(pair, carry):
        own = pair_sum(pair, low_ref[pair], table_ref, slot_ref)
        total = own + other_ref[pair].astype(jnp.float32)
        ar = ar_ref[pair]
        half = half_ref[pair]
        turned = []
        parts = []
        sum_coef = jnp.zeros((steps, LANES), jnp.float32)
        sum_var = jnp.zeros((steps, LANES), jnp.float32)
        for part in range(2):
            spectral = total[:, part * days : (part + 1) * days]
            parts.append(spectral)
            previous = jnp.where(lane == 0, 0.0, pltpu.roll(spectral, 1, 1))
            residual = spectral - ar * previous
            scaled = residual * season_ref[0:1, :]
            innovation = (scaled * half).astype(jnp.bfloat16)
            turned.append(
                lax.dot_general(turn, innovation, transposed, preferred_element_type=jnp.float32)
            )
            weighted = residual * season_ref[1:2, :]
            sum_coef = sum_coef + weighted * previous
            sum_var = sum_var + weighted * residual
        sum_coef = jnp.sum(sum_coef, axis=1, keepdims=True)
        sum_var = jnp.sum(sum_var, axis=1, keepdims=True)
        misc = jnp.where(
            (lane == 0) | (lane == LANES - 1),
            parts[0],
            jnp.where(lane < 3, pltpu.roll(parts[1], 2, 1), jnp.where(lane == 3, sum_coef, sum_var)),
        )
        misc_high = misc.astype(jnp.bfloat16)
        misc_low = (misc - misc_high.astype(jnp.float32)).astype(jnp.bfloat16)
        for piece in (misc_high, misc_low):
            turned.append(lax.dot_general(pick, piece, transposed, preferred_element_type=jnp.float32))
        stacked = jnp.concatenate(turned, axis=0).astype(jnp.bfloat16)
        row = lax.broadcasted_iota(jnp.int32, (steps, degrees), 0)
        degree = lax.broadcasted_iota(jnp.int32, (steps, degrees), 1)
        for position in range(2):
            slot = 2 * pair + position
            chosen = (row - degree == shift_ref[slot]) & (degree >= wave_ref[slot])
            placed = jnp.dot(stacked, chosen.astype(jnp.bfloat16), preferred_element_type=jnp.float32)
            for part in range(2):
                for t in range(lane_tiles):
                    turned_ref[part, t, pl.ds(slot, days, stride=TILE), :] = placed[
                        part * days : (part + 1) * days, t * LANES : (t + 1) * LANES
                    ]
            misc_ref[slot] = placed[2 * days : 2 * days + 8] + placed[2 * days + 8 : 2 * days + 16]
        return carry

    lax.fori_loop(0, TILE // 2, one, 0)

    def write(day, carry):
        for part in range(2):
            for t in range(lane_tiles):
                values = turned_ref[part, t, pl.ds(pl.multiple_of(day * TILE, TILE), TILE), :]
                out_ref[day, part, :, t * LANES : (t + 1) * LANES] = values.astype(jnp.bfloat16)
        return carry

    lax.fori_loop(0, days, write, 0)


def leading(shape, chunk):
    return pl.BlockSpec(shape, lambda i: (chunk,) + (0,) * (len(shape) - 1))


def partial_sums(chunk, low, block, table):
    sources, lats, rows, days = block.shape
    steps = table.shape[1]
    lat_half = sources * lats
    pairs = TILE // 2
    return pl.pallas_call(
        partial_kernel,
        grid=(1,),
        in_specs=[
            pl.BlockSpec(memory_space=pltpu.SMEM),
            leading(block.shape, 0),
            leading((pairs, steps, lat_half), chunk),
        ],
        out_specs=leading((pairs, steps, 2 * days), 0),
        out_shape=jax.ShapeDtypeStruct((pairs, steps, 2 * days), jnp.bfloat16),
        scratch_shapes=[
            pltpu.VMEM((lat_half * TILE, days), jnp.float32),
            pltpu.VMEM((TILE, lat_half, 2 * days), jnp.bfloat16),
        ],
        compiler_params=pltpu.CompilerParams(vmem_limit_bytes=VMEM_LIMIT),
        cost_estimate=pl.CostEstimate(
            flops=2 * TILE * steps * lat_half * 2 * days, bytes_accessed=8 * 1024 * 1024, transcendentals=0
        ),
    )(low, block, table)


def finish(chunk, first, low, waves, shifts, block, table, other, ar, half, season, held, slot_total):
    sources, lats, rows, days = block.shape
    steps = table.shape[1]
    lat_half = sources * lats
    pairs = TILE // 2
    smem = pl.BlockSpec(memory_space=pltpu.SMEM)
    operands = [low, waves, shifts, block, table, other, ar[chunk], half[chunk], season]
    in_specs = [
        smem,
        smem,
        smem,
        leading(block.shape, 0),
        leading((pairs, steps, lat_half), first + chunk),
        leading((pairs, steps, 2 * days), 0),
        leading((pairs, steps, LANES), 0),
        leading((pairs, steps, LANES), 0),
        leading((8, LANES), 0),
    ]
    aliases = {}
    if held is not None:
        operands.append(held)
        in_specs.append(pl.BlockSpec(memory_space=pl.ANY))
        aliases = {len(operands) - 1: 0}
    degree_count = slot_total[1]
    return pl.pallas_call(
        finish_kernel,
        grid=(1,),
        in_specs=in_specs,
        out_specs=[
            pl.BlockSpec((days, 2, TILE, degree_count), lambda i: (0, 0, chunk, 0)),
            leading((TILE, 8, degree_count), 0),
        ],
        out_shape=[
            jax.ShapeDtypeStruct((days, 2, slot_total[0], degree_count), jnp.bfloat16),
            jax.ShapeDtypeStruct((TILE, 8, degree_count), jnp.float32),
        ],
        input_output_aliases=aliases,
        scratch_shapes=[
            pltpu.VMEM((lat_half * TILE, days), jnp.float32),
            pltpu.VMEM((TILE, lat_half, 2 * days), jnp.bfloat16),
            pltpu.VMEM((2, degree_count // LANES, days * TILE, LANES), jnp.float32),
        ],
        compiler_params=pltpu.CompilerParams(vmem_limit_bytes=VMEM_LIMIT),
        cost_estimate=pl.CostEstimate(
            flops=4 * TILE * steps * lat_half * 2 * days, bytes_accessed=12 * 1024 * 1024, transcendentals=0
        ),
    )(*operands)


def pack_rows(values, low, steps):
    degrees = values.shape[2]
    row = jnp.arange(steps, dtype=jnp.int32)[None, :]
    first = row <= low[:, None]
    source = jnp.where(first, row + (degrees - 1) - low[:, None], degrees + row - 1)
    source = jnp.clip(source, 0, 2 * degrees - 1)
    return jnp.take_along_axis(values.reshape(values.shape[0], 2 * degrees), source, axis=1)


def per_device(fields, wave_table, day_of_year, ar_coef, log_var):
    band_count = lax.axis_size("band")
    time_count = lax.axis_size("tm")
    band = lax.axis_index("band")
    slot_count, degree_count = ar_coef.shape
    day_count, lat_local, lon_count = fields.shape
    lat_count = lat_local * band_count
    group = band_count // 2
    lat_half = lat_local * group
    steps = round_up(degree_count + 1, TILE)
    total_days = day_count * time_count
    slot_pad = round_up(slot_count, TILE)
    chunks = slot_pad // TILE
    pairs = slot_pad // 2
    half_index = band // group
    rank = band % group
    half_groups = [list(range(group)), list(range(group, band_count))]
    mirror = [(i, (i + group) % band_count) for i in range(band_count)]

    waves = wave_table.reshape(2, group, slot_count // 2, 2)
    high_low = jnp.stack([waves.max(-1), waves.min(-1)], axis=-1)
    high_low = jnp.pad(high_low, ((0, 0), (0, 0), (0, pairs - slot_count // 2), (0, 0)))
    present = jnp.arange(slot_pad) < slot_count
    ordered = high_low.reshape(2, group, chunks, TILE)
    own_order = lax.dynamic_index_in_dim(ordered, half_index, 0, keepdims=False)
    far_order = lax.dynamic_index_in_dim(ordered, 1 - half_index, 0, keepdims=False)

    def low_waves(order):
        return lax.dynamic_index_in_dim(order, rank, 0, keepdims=False).reshape(pairs, 2)[:, 1]

    own_low, far_low = low_waves(own_order), low_waves(far_order)
    lows = jnp.concatenate([far_low, own_low])
    lows = jnp.pad(lows, (0, round_up(2 * pairs, TILE) - 2 * pairs))

    def transform(order, first, count):
        picked = order[:, first : first + count].reshape(-1)
        cosine, minus_sine = fourier_columns(picked, lon_count)
        shape = (lon_count, group, count, 1, TILE)
        table = jnp.concatenate([cosine.reshape(shape), minus_sine.reshape(shape)], axis=3)
        if slot_pad != slot_count:
            mask = present.reshape(chunks, TILE)[first : first + count]
            table = table * mask[None, None, :, None, :]
        table = table.astype(jnp.bfloat16).reshape(lon_count, group * count * 2 * TILE)
        coeffs = jnp.einsum("djk,kq->jqd", fields, table, preferred_element_type=jnp.float32)
        coeffs = coeffs.astype(jnp.bfloat16).reshape(lat_local, group, count, 2 * TILE, day_count)
        return [coeffs[:, :, i].transpose(1, 0, 2, 3) for i in range(count)]

    def exchange(block):
        return lax.all_to_all(block, "band", 0, 0, axis_index_groups=half_groups, tiled=True)

    far_blocks = transform(far_order, 0, 1)
    if chunks > 1:
        far_blocks = far_blocks + transform(far_order, 1, chunks - 1)
    own_blocks = transform(own_order, 0, chunks)
    table = packed_table(lows, half_index * lat_half, lat_half, lat_count, degree_count, steps)

    others = []
    for chunk in range(chunks):
        block = exchange(far_blocks[chunk])
        low = far_low[chunk * TILE // 2 : (chunk + 1) * TILE // 2]
        sums = partial_sums(chunk, low, block, table)
        others.append(lax.ppermute(sums, "band", mirror))

    own_waves = lax.dynamic_slice_in_dim(wave_table, band * slot_count, slot_count)
    pad_slots = ((0, slot_pad - slot_count),)
    slot_waves = jnp.pad(own_waves, pad_slots)
    is_low = (slot_waves.reshape(pairs, 2) == own_low[:, None])
    first_low = is_low[:, 0]
    shifts = jnp.where(is_low, 1, -slot_waves.reshape(pairs, 2)).reshape(slot_pad)

    def by_pair(values):
        values = jnp.pad(values, pad_slots + ((0, 0),)).reshape(pairs, 2, degree_count)
        return jnp.where(first_low[:, None, None], values[:, ::-1], values)

    def spread_rows(values):
        packed = pack_rows(by_pair(values), own_low, steps)
        packed = jnp.broadcast_to(packed[:, :, None], (pairs, steps, LANES))
        return packed.reshape(chunks, TILE // 2, steps, LANES)

    ar_rows = spread_rows(ar_coef)
    half_rows = spread_rows(jnp.exp(-0.5 * log_var))
    season = 1.0 + 0.5 * jnp.cos(day_of_year.astype(jnp.float32) * (2.0 * math.pi / 365.0))
    later = (jnp.arange(day_count) > 0).astype(jnp.float32)
    season_rows = jnp.stack([lax.rsqrt(season), later / season])
    season_rows = jnp.pad(season_rows, ((0, 6), (0, 0)))

    innovation = None
    misc = []
    for chunk in range(chunks):
        block = exchange(own_blocks[chunk])
        low = own_low[chunk * TILE // 2 : (chunk + 1) * TILE // 2]
        span = slice(chunk * TILE, (chunk + 1) * TILE)
        innovation, rows = finish(
            chunk, chunks, low, slot_waves[span], shifts[span], block, table, others[chunk],
            ar_rows, half_rows, season_rows, innovation, (slot_pad, degree_count),
        )
        misc.append(rows)
    innovation = innovation[:, :, :slot_count]
    misc = jnp.concatenate(misc, axis=0)[:slot_count].transpose(1, 0, 2)
    first_day, last_day = misc[0:2], misc[2:4]
    route = [(i, i + 1) for i in range(time_count - 1)]
    carried = lax.ppermute(last_day.astype(jnp.bfloat16), "tm", route).astype(jnp.float32)

    degree_list = jnp.arange(degree_count, dtype=jnp.int32)
    valid_mask = (degree_list[None, :] >= own_waves[:, None]).astype(jnp.float32)
    variance = jnp.exp(-log_var)
    residual = first_day - ar_coef[None] * carried
    inverse = variance / season[0]
    opening = (residual * jnp.sqrt(inverse)[None] * valid_mask[None]).astype(jnp.bfloat16)
    innovation = lax.dynamic_update_slice_in_dim(innovation, opening[None], 0, 0)
    sum_coef = misc[4] * variance + jnp.sum(residual * carried, axis=0) * inverse
    sum_var = day_count - 0.5 * (misc[5] * variance + jnp.sum(residual * residual, axis=0) * inverse)
    sums = jnp.stack([sum_coef, sum_var]).astype(jnp.bfloat16)
    column_width = degree_count // time_count
    sums = sums.reshape(2, slot_count, time_count, column_width).transpose(2, 0, 1, 3)
    sums = lax.all_to_all(sums, "tm", 0, 0, tiled=True)
    sums = jnp.sum(sums.astype(jnp.float32), axis=0)
    local_mask = lax.dynamic_slice_in_dim(valid_mask, lax.axis_index("tm") * column_width, column_width, 1)
    grad_coef = -local_mask * sums[0] / (2.0 * total_days)
    grad_var = local_mask * sums[1] / (2.0 * total_days)
    return innovation, grad_coef, grad_var


def solution(mesh):
    in_specs = (P("tm", "band", None), P(), P("tm"), P("band", None), P("band", None))
    out_specs = (P("tm", None, "band", None), P("band", "tm"), P("band", "tm"))
    return jax.shard_map(
        per_device, mesh=mesh, in_specs=in_specs, out_specs=out_specs, check_vma=False
    )
```

time: 597 us -> 632 us (1.059)
  Pallas kernels: 0 us -> 127 us
  other arithmetic: 143 us -> 20 us
  local copies, waits for them, and re-layouts: 102 us -> 215 us
  waiting for transfers between devices: 251 us -> 168 us
  starting transfers between devices: 8.66 us -> 41.2 us
  matrix products: 67.5 us -> 53 us
  between operations: 14.2 us -> 1.64 us
  loops' own time: 10.5 us -> 0 us
    gather x0 -> x5, local copies, waits for them, and re-layouts: none -> 146 us  [pack_rows(): jnp.take_along_axis(values.reshape(values.shape[0], 2 * degrees), source,...]
    all_to_all x1 -> x7, waiting for transfers between devices: 221 us -> 91.2 us  [the longest x6 87.5 us: exchange(): lax.all_to_all(block, 'band', 0, 0, axis_index_groups=half_groups, tiled=...]
    pallas_call x0 -> x7, Pallas kernels: none -> 127 us  [the longest x3 67.7 us: finish(): pl.pallas_call(finish_kernel, grid=(1,), in_specs=in_specs, out_specs=[pl...]
    while x360 -> x0, other arithmetic: 80.3 us -> none
    ppermute x1 -> x4, waiting for transfers between devices: 0.82 us -> 76.5 us  [the longest x3 75.8 us: per_device(): others.append(lax.ppermute(sums, 'band', mirror))]
    reshape x1 -> x6, local copies, waits for them, and re-layouts: 32.1 us -> 1.15 us  [the longest x1 0.82 us: per_device(): waves = wave_table.reshape(2, group, slot_count // 2, 2)]
    unnamed x4 -> x0, waiting for transfers between devices: 29.7 us -> none
    all_to_all x1 -> x7, starting transfers between devices: 7.28 us -> 34.3 us  [the longest x6 28 us: exchange(): lax.all_to_all(block, 'band', 0, 0, axis_index_groups=half_groups, tiled=...]
  transfers between devices with their start and end apart: 4 -> 11, of which waited for: 4 -> 7; matrix products, arithmetic and copies ran while one was open for 26% -> 41% of each run, Pallas kernels for 0% -> 17%
where the time goes in v1:
time: 632 us; the launch traced here: 625 us
  local copies, waits for them, and re-layouts  215 us (34%)
  waiting for transfers between devices  168 us (27%)
  Pallas kernels  127 us (20%)
  matrix products  53 us (8%)
  starting transfers between devices  41.2 us (7%)
  other arithmetic  20 us (3%)
    gather x5, local copies, waits for them, and re-layouts, pack_rows(): jnp.take_along_axis(values.reshape(values.shape[0], 2 * degrees), source,...  146 us
    all_to_all x6, waiting for transfers between devices, exchange(): lax.all_to_all(block, 'band', 0, 0, axis_index_groups=half_groups, tiled=...  87.5 us
    ppermute x3, waiting for transfers between devices, per_device(): others.append(lax.ppermute(sums, 'band', mirror))  75.8 us
    pallas_call x3, Pallas kernels, finish(): pl.pallas_call(finish_kernel, grid=(1,), in_specs=in_specs, out_specs=[pl...  67.7 us
    dot_general x3, matrix products, transform(): jnp.einsum('djk,kq->jqd', fields, table, preferred_element_type=jnp.float32)  53 us
    pallas_call x3, Pallas kernels, partial_sums(): pl.pallas_call(partial_kernel, grid=(1,), in_specs=[pl.BlockSpec(memory_s...  29.5 us
    pallas_call x1, Pallas kernels, packed_table(): pl.pallas_call(functools.partial(table_kernel, steps, lane_tiles, top), g...  29.3 us
    all_to_all x6, starting transfers between devices, exchange(): lax.all_to_all(block, 'band', 0, 0, axis_index_groups=half_groups, tiled=...  28 us
  transfers between devices with their start and end apart: 11, of which 7 were waited for; matrix products, arithmetic and copies ran while one was open for 41% of the time, Pallas kernels for 17%

profile of v1, /device:TPU:0, one launch (start us, length us, event | category | flops | bytes accessed | tf_op | source)
XLA Modules:
  0.0 625.2 jit_solution(12321563350815865856)
XLA Ops:
  0.7 0.8 reshape.1061
  2.6 1.0 subtract_convert_fusion.2
  4.3 0.7 sub.118
  5.1 14.9 %convolution_convert_fusion.2 = bf16[128,128,88]{1,0,2:T(8,128)(2,1)S(1)} fusion(bf16[1440,128,1]{0,1,2:T(8,128)(2,1)S(1)} %bitcast.126, bf16[128,88,1440]{0,2,1:T(8,128)(2,1)} %param.7), kind=kOutput, calls=%fused_computation.14 | convolution fusion | flops 4153802752 | bytes 35692544 | tf_op jit(solution)/shard_map/djk,kq->jqd/dot_general | solution.py:402
  19.9 2.2 copy.104
  22.1 5.5 all-to-all-start.5
  28.8 4.6 subtract_convert_fusion
  33.3 3.6 neg.52
  36.9 4.3 sub.107
  41.3 1.2 pad_maximum_fusion
  42.4 1.1 copy.51
  43.6 21.7 %convolution_convert_fusion = bf16[384,128,88]{1,0,2:T(8,128)(2,1)} fusion(bf16[1440,384,1]{0,1,2:T(8,128)(2,1)} %bitcast.127, bf16[128,88,1440]{0,2,1:T(8,128)(2,1)} %param.7), kind=kOutput, calls=%fused_computation.2 | convolution fusion | flops 12461408256 | bytes 42196992 | tf_op jit(solution)/shard_map/djk,kq->jqd/dot_general | solution.py:402
  65.2 6.7 %fusion.81 = (bf16[88,4,1,32,128]{4,3,2,1,0:T(8,128)(2,1)S(1)}, bf16[88,4,1,32,128]{4,3,2,1,0:T(8,128)(2,1)}, bf16[88,4,1,32,128]{4,3,2,1,0:T(8,128)(2,1)}) fusion(bf16[88,4,3,32,128]{4,3,2,1,0:T(8,128)(2,1)} %bitcast.124), kind=kLoop, calls=%fused_computation.221 | loop fusion | bytes 17301504 | tf_op jit(solution)/shard_map/slice | solution.py:404
  71.9 2.1 copy.99
  74.0 1.6 copy-done.1
  75.6 4.6 all-to-all-start.4
  81.0 3.2 subtract_convert_fusion.1
  84.3 2.6 neg.54
  86.9 3.3 sub.114
  90.2 1.1 pad_maximum_fusion.1
  91.4 16.5 %convolution_convert_fusion.1 = bf16[256,128,88]{1,0,2:T(8,128)(2,1)} fusion(bf16[1440,256,1]{0,1,2:T(8,128)(2,1)S(1)} %bitcast.128, bf16[128,88,1440]{0,2,1:T(8,128)(2,1)} %param.7), kind=kOutput, calls=%fused_computation.5 | convolution fusion | flops 8307605504 | bytes 38944768 | tf_op jit(solution)/shard_map/djk,kq->jqd/dot_general | solution.py:402
  107.9 6.8 %fusion.82 = (bf16[88,4,1,32,128]{4,3,2,1,0:T(8,128)(2,1)S(1)}, bf16[88,4,1,32,128]{4,3,2,1,0:T(8,128)(2,1)}) fusion(bf16[88,4,2,32,128]{4,3,2,1,0:T(8,128)(2,1)} %bitcast.125), kind=kLoop, calls=%fused_computation.222 | loop fusion | bytes 11534336 | tf_op jit(solution)/shard_map/slice | solution.py:404
  114.6 2.1 copy.100
  116.7 4.7 all-to-all-start.3
  121.4 4.0 copy.101
  125.4 28.9 %all-to-all-done.3.in_ref = bf16[4,88,32,128]{3,2,1,0:T(8,128)(2,1)} async-done(((bf16[4,88,32,128]{3,2,1,0:T(8,128)(2,1)}), bf16[4,88,32,128]{3,2,1,0:T(8,128)(2,1)}, u32[]{:S(2)}, u32[]{:S(2)}) %all-to-all-start.3) | async-done | bytes 2883616 | tf_op jit(solution)/shard_map/all_to_all | solution.py:407
  154.3 4.9 all-to-all-start.2
  159.1 2.1 copy.102
  161.3 31.4 %all-to-all-done.2.in_ref = bf16[4,88,32,128]{3,2,1,0:T(8,128)(2,1)} async-done(((bf16[4,88,32,128]{3,2,1,0:T(8,128)(2,1)}), bf16[4,88,32,128]{3,2,1,0:T(8,128)(2,1)}, u32[]{:S(2)}, u32[]{:S(2)}) %all-to-all-start.2) | async-done | bytes 2883616 | tf_op jit(solution)/shard_map/all_to_all | solution.py:407
  192.7 3.7 all-to-all-start.1
  196.8 3.9 copy.103
  201.8 27.2 %all-to-all-done.1.in_ref = bf16[4,88,32,128]{3,2,1,0:T(8,128)(2,1)S(1)} async-done(((bf16[4,88,32,128]{3,2,1,0:T(8,128)(2,1)}), bf16[4,88,32,128]{3,2,1,0:T(8,128)(2,1)S(1)}, u32[]{:S(2)}, u32[]{:S(2)}) %all-to-all-start.1) | async-done | bytes 2883616 | tf_op jit(solution)/shard_map/all_to_all | solution.py:407
  229.0 4.8 all-to-all-start
  234.0 0.8 dynamic_slice.21
  235.6 0.8 multiply_add_fusion
  236.4 0.7 broadcast_in_dim.46.low_ref
  238.2 29.3 %shard_map.76.table_ref = bf16[48,400,352]{2,1,0:T(8,128)(2,1)} custom-call(f32[48,128]{1,0:T(8,128)} %broadcast_in_dim.46.low_ref, f32[48,384]{1,0:T(8,128)} %get-tuple-element.66.first_ref, f32[48,384]{1,0:T(8,128)} %get-tuple-element.65.second_ref, f32[16,384]{1,0:T(8,128)} %broadcast_in_dim.47.cos_ref, f32[16,384]{1,0:T(8,128)} %broadcast_in_dim.51.weight_ref), custom_call_target="tpu_custom_call" | custom-call | flops 88473600 | bytes 14745600 | tf_op jit(solution)/shard_map/pallas_call | solution.py:138
  267.6 0.8 slice_reduce_fusion.3
  268.9 9.8 %shard_map.79 = bf16[8,400,256]{2,1,0:T(8,128)(2,1)} custom-call(s32[8]{0:T(128)} %get-tuple-element.22.low_ref, bf16[4,88,32,128]{3,2,1,0:T(8,128)(2,1)} %copy-done.1, bf16[48,400,352]{2,1,0:T(8,128)(2,1)} %shard_map.76.table_ref), custom_call_target="tpu_custom_call" | custom-call | flops 1153433600 | bytes 8388608 | tf_op jit(solution)/shard_map/pallas_call | solution.py:280
  278.7 2.7 collective-permute-start.2
  282.1 72.6 %gather_fusion = f32[9600]{0:T(1024)S(1)} fusion(f32[24,768]{1,0:T(8,128)S(1)} %bitcast.121, s32[9600]{0:T(1024)S(1)} %reshape.1096), kind=kCustom, calls=%fused_computation.clone | custom fusion | bytes 153600 | tf_op jit(solution)/shard_map/jit(take_along_axis)/gather | solution.py:356
  354.7 0.7 reshape.1099
  355.4 72.6 %gather_fusion.1 = f32[9600]{0:T(1024)S(1)} fusion(f32[24,768]{1,0:T(8,128)S(1)} %bitcast.122, s32[9600]{0:T(1024)S(1)} %reshape.1096), kind=kCustom, calls=%fused_computation.1.clone | custom fusion | bytes 153600 | tf_op jit(solution)/shard_map/jit(take_along_axis)/gather | solution.py:356
  430.0 10.0 %shard_map.78 = bf16[8,400,256]{2,1,0:T(8,128)(2,1)} custom-call(s32[8]{0:T(128)} %get-tuple-element.23.low_ref, bf16[4,88,32,128]{3,2,1,0:T(8,128)(2,1)} %all-to-all-done.3.in_ref, bf16[48,400,352]{2,1,0:T(8,128)(2,1)} %shard_map.76.table_ref), custom_call_target="tpu_custom_call" | custom-call | flops 1153433600 | bytes 8388608 | tf_op jit(solution)/shard_map/pallas_call | solution.py:280
  440.2 0.8 slice_reduce_fusion.4
  441.0 9.8 %shard_map.77 = bf16[8,400,256]{2,1,0:T(8,128)(2,1)} custom-call(s32[8]{0:T(128)} %get-tuple-element.24.low_ref, bf16[4,88,32,128]{3,2,1,0:T(8,128)(2,1)} %copy-done.2, bf16[48,400,352]{2,1,0:T(8,128)(2,1)} %shard_map.76.table_ref), custom_call_target="tpu_custom_call" | custom-call | flops 1153433600 | bytes 8388608 | tf_op jit(solution)/shard_map/pallas_call | solution.py:280
  450.8 2.8 collective-permute-start
  454.9 1.8 broadcast_in_dim.59.ar_ref
  456.7 1.7 broadcast_in_dim.60.half_ref
  458.4 22.7 %shard_map.80 = (bf16[128,2,48,384]{3,2,1,0:T(8,128)(2,1)}, f32[16,8,384]{2,1,0:T(8,128)}) custom-call(s32[8]{0:T(128)} %get-tuple-element.25.low_ref, s32[16]{0:T(128)} %get-tuple-element.77.wave_ref, s32[16]{0:T(128)} %slice.181.shift_ref, bf16[4,88,32,128]{3,2,1,0:T(8,128)(2,1)} %copy-done, bf16[48,400,352]{2,1,0:T(8,128)(2,1)} %shard_map.76.table_ref, ...), custom_call_target="tpu_custom_call" | custom-call | flops 2306867200 | bytes 12582912 | tf_op jit(solution)/shard_map/pallas_call | solution.py:325
  481.1 68.6 %collective-permute-done.1.other_ref = bf16[8,400,256]{2,1,0:T(8,128)(2,1)S(1)} collective-permute-done((bf16[8,400,256]{2,1,0:T(8,128)(2,1)}, bf16[8,400,256]{2,1,0:T(8,128)(2,1)S(1)}, u32[]{:S(2)}, u32[]{:S(2)}) %collective-permute-start.1) | collective-permute-done | bytes 1638432 | tf_op jit(solution)/shard_map/ppermute | solution.py:420
  549.7 1.8 broadcast_in_dim.57.ar_ref
  551.5 1.7 broadcast_in_dim.58.half_ref
  553.1 22.5 %shard_map.81 = (bf16[128,2,48,384]{3,2,1,0:T(8,128)(2,1)}, f32[16,8,384]{2,1,0:T(8,128)}) custom-call(s32[8]{0:T(128)} %get-tuple-element.26.low_ref, s32[16]{0:T(128)} %get-tuple-element.78.wave_ref, s32[16]{0:T(128)} %slice.170.shift_ref, bf16[4,88,32,128]{3,2,1,0:T(8,128)(2,1)} %all-to-all-done.2.in_ref, ...), custom_call_target="tpu_custom_call", output_to_operand_aliasing={{0}: (9, {})} | custom-call | flops 2306867200 | bytes 12582912 | tf_op jit(solution)/shard_map/pallas_call | solution.py:325
  575.6 7.2 %collective-permute-done.other_ref = bf16[8,400,256]{2,1,0:T(8,128)(2,1)S(1)} collective-permute-done((bf16[8,400,256]{2,1,0:T(8,128)(2,1)}, bf16[8,400,256]{2,1,0:T(8,128)(2,1)S(1)}, u32[]{:S(2)}, u32[]{:S(2)}) %collective-permute-start) | collective-permute-done | bytes 1638432 | tf_op jit(solution)/shard_map/ppermute | solution.py:420
  582.8 1.8 broadcast_in_dim.55.ar_ref
  584.6 1.7 broadcast_in_dim.56.half_ref
  586.3 22.5 %shard_map.82 = (bf16[128,2,48,384]{3,2,1,0:T(8,128)(2,1)}, f32[16,8,384]{2,1,0:T(8,128)}) custom-call(s32[8]{0:T(128)} %get-tuple-element.27.low_ref, s32[16]{0:T(128)} %get-tuple-element.79.wave_ref, s32[16]{0:T(128)} %slice.156.shift_ref, bf16[4,88,32,128]{3,2,1,0:T(8,128)(2,1)} %all-to-all-done.in_ref, ...), custom_call_target="tpu_custom_call", output_to_operand_aliasing={{0}: (9, {})} | custom-call | flops 2306867200 | bytes 12582912 | tf_op jit(solution)/shard_map/pallas_call | solution.py:325
  608.8 1.0 maximum_bitcast_fusion
  609.9 1.3 collective-permute-start.3
  611.3 0.8 collective-permute-done.3
  613.5 6.2 all-to-all-start.6
  620.4 3.7 all-to-all-done.6
  624.1 0.7 fusion.59
  (108 shorter events, 14.5 us)
Async XLA Ops:
  22.1 51.9 %all-to-all-start.5 = ((bf16[4,88,32,128]{3,2,1,0:T(8,128)(2,1)}), bf16[4,88,32,128]{3,2,1,0:T(8,128)(2,1)S(1)}, u32[]{:S(2)}, u32[]{:S(2)}) async-start(bf16[4,88,32,128]{3,2,1,0:T(8,128)(2,1)} %bitcast.119), calls=%async_computation.5 | async-start | bytes 5767168 | tf_op jit(solution)/shard_map/all_to_all | solution.py:407
  74.0 1.6 copy-start.1
  75.6 41.1 %all-to-all-start.4 = ((bf16[4,88,32,128]{3,2,1,0:T(8,128)(2,1)}), bf16[4,88,32,128]{3,2,1,0:T(8,128)(2,1)S(1)}, u32[]{:S(2)}, u32[]{:S(2)}) async-start(bf16[4,88,32,128]{3,2,1,0:T(8,128)(2,1)} %bitcast.114), calls=%async_computation.4 | async-start | bytes 5767168 | tf_op jit(solution)/shard_map/all_to_all | solution.py:407
  116.7 8.6 %copy-start = (bf16[4,88,32,128]{3,2,1,0:T(8,128)(2,1)}, bf16[4,88,32,128]{3,2,1,0:T(8,128)(2,1)S(1)}, u32[]{:S(2)}) copy-start(bf16[4,88,32,128]{3,2,1,0:T(8,128)(2,1)S(1)} %all-to-all-done.4.in_ref) | copy-start | bytes 8650756
  116.7 37.5 %all-to-all-start.3 = ((bf16[4,88,32,128]{3,2,1,0:T(8,128)(2,1)}), bf16[4,88,32,128]{3,2,1,0:T(8,128)(2,1)}, u32[]{:S(2)}, u32[]{:S(2)}) async-start(bf16[4,88,32,128]{3,2,1,0:T(8,128)(2,1)} %bitcast.115), calls=%async_computation.3 | async-start | bytes 5767168 | tf_op jit(solution)/shard_map/all_to_all | solution.py:407
  154.3 4.9 copy-start.3
  154.3 38.4 %all-to-all-start.2 = ((bf16[4,88,32,128]{3,2,1,0:T(8,128)(2,1)}), bf16[4,88,32,128]{3,2,1,0:T(8,128)(2,1)}, u32[]{:S(2)}, u32[]{:S(2)}) async-start(bf16[4,88,32,128]{3,2,1,0:T(8,128)(2,1)} %bitcast.116), calls=%async_computation.2 | async-start | bytes 5767168 | tf_op jit(solution)/shard_map/all_to_all | solution.py:407
  192.7 36.4 %all-to-all-start.1 = ((bf16[4,88,32,128]{3,2,1,0:T(8,128)(2,1)}), bf16[4,88,32,128]{3,2,1,0:T(8,128)(2,1)S(1)}, u32[]{:S(2)}, u32[]{:S(2)}) async-start(bf16[4,88,32,128]{3,2,1,0:T(8,128)(2,1)} %bitcast.117), calls=%async_computation.1 | async-start | bytes 5767168 | tf_op jit(solution)/shard_map/all_to_all | solution.py:407
  196.4 4.7 copy-start.15
  196.4 5.3 copy-start.7
  201.7 33.4 %copy-start.8 = (f32[48,384]{1,0:T(8,128)S(1)}, f32[48,384]{1,0:T(8,128)}, u32[]{:S(2)}) copy-start(f32[48,384]{1,0:T(8,128)} %param.10) | copy-start | bytes 221188
  229.0 6.5 %copy-start.2 = (bf16[4,88,32,128]{3,2,1,0:T(8,128)(2,1)}, bf16[4,88,32,128]{3,2,1,0:T(8,128)(2,1)S(1)}, u32[]{:S(2)}) copy-start(bf16[4,88,32,128]{3,2,1,0:T(8,128)(2,1)S(1)} %all-to-all-done.1.in_ref) | copy-start | bytes 8650756
  229.0 346.6 %all-to-all-start = ((bf16[4,88,32,128]{3,2,1,0:T(8,128)(2,1)}), bf16[4,88,32,128]{3,2,1,0:T(8,128)(2,1)}, u32[]{:S(2)}, u32[]{:S(2)}) async-start(bf16[4,88,32,128]{3,2,1,0:T(8,128)(2,1)} %bitcast.118), calls=%async_computation | async-start | bytes 5767168 | tf_op jit(solution)/shard_map/all_to_all | solution.py:407
  278.7 176.2 %collective-permute-start.2 = (bf16[8,400,256]{2,1,0:T(8,128)(2,1)}, bf16[8,400,256]{2,1,0:T(8,128)(2,1)S(1)}, u32[]{:S(2)}, u32[]{:S(2)}) collective-permute-start(bf16[8,400,256]{2,1,0:T(8,128)(2,1)} %shard_map.79), channel_id=1, source_target_pairs={{0,16},{4,20},{8,24},{12,28},{16,0},{20,4},{24,8},{28,12},{1,17},{... | collective-permute-start | bytes 4915208 | tf_op jit(solution)/shard_map/ppermute | solution.py:420
  440.0 109.7 %collective-permute-start.1 = (bf16[8,400,256]{2,1,0:T(8,128)(2,1)}, bf16[8,400,256]{2,1,0:T(8,128)(2,1)S(1)}, u32[]{:S(2)}, u32[]{:S(2)}) collective-permute-start(bf16[8,400,256]{2,1,0:T(8,128)(2,1)} %shard_map.78), channel_id=1, source_target_pairs={{0,16},{4,20},{8,24},{12,28},{16,0},{20,4},{24,8},{28,12},{1,17},{... | collective-permute-start | bytes 4915208 | tf_op jit(solution)/shard_map/ppermute | solution.py:420
  441.0 12.5 %copy-start.13 = (f32[1,128]{1,0:T(1,128)S(1)}, f32[1,128]{1,0:T(1,128)}, u32[]{:S(2)}) copy-start(f32[1,128]{1,0:T(1,128)} %get-tuple-element.28) | copy-start | bytes 1540
  441.0 12.5 %copy-start.14 = (f32[1,128]{1,0:T(1,128)S(1)}, f32[1,128]{1,0:T(1,128)}, u32[]{:S(2)}) copy-start(f32[1,128]{1,0:T(1,128)} %fusion.79) | copy-start | bytes 1540
  441.0 13.7 %copy-start.12 = (f32[24,400]{1,0:T(8,128)S(1)}, f32[24,400]{1,0:T(8,128)}, u32[]{:S(2)}) copy-start(f32[24,400]{1,0:T(8,128)} %reshape.1099) | copy-start | bytes 115204
  450.8 132.0 %collective-permute-start = (bf16[8,400,256]{2,1,0:T(8,128)(2,1)}, bf16[8,400,256]{2,1,0:T(8,128)(2,1)S(1)}, u32[]{:S(2)}, u32[]{:S(2)}) collective-permute-start(bf16[8,400,256]{2,1,0:T(8,128)(2,1)} %shard_map.77), channel_id=1, source_target_pairs={{0,16},{4,20},{8,24},{12,28},{16,0},{20,4},{24,8},{28,12},{1,17},{... | collective-permute-start | bytes 4915208 | tf_op jit(solution)/shard_map/ppermute | solution.py:420
  454.9 3.5 copy-start.4
  549.7 3.4 copy-start.6
  582.8 3.5 copy-start.5
  586.3 22.6 %copy-start.10 = (f32[16,8,384]{2,1,0:T(8,128)S(1)}, f32[16,8,384]{2,1,0:T(8,128)}, u32[]{:S(2)}) copy-start(f32[16,8,384]{2,1,0:T(8,128)} %get-tuple-element.13) | copy-start | bytes 589828
  586.3 22.6 %copy-start.11 = (f32[16,8,384]{2,1,0:T(8,128)S(1)}, f32[16,8,384]{2,1,0:T(8,128)}, u32[]{:S(2)}) copy-start(f32[16,8,384]{2,1,0:T(8,128)} %get-tuple-element.14) | copy-start | bytes 589828
  586.3 25.8 %copy-start.9 = (f32[48,384]{1,0:T(8,128)S(1)}, f32[48,384]{1,0:T(8,128)}, u32[]{:S(2)}) copy-start(f32[48,384]{1,0:T(8,128)} %param.10) | copy-start | bytes 221188
  609.9 2.2 collective-permute-start.3
  613.5 10.5 %all-to-all-start.6 = ((bf16[4,2,48,96]{3,2,1,0:T(8,128)(2,1)}), bf16[4,2,48,96]{3,2,1,0:T(8,128)(2,1)S(1)}, u32[]{:S(2)}, u32[]{:S(2)}) async-start(bf16[4,2,48,96]{3,2,1,0:T(8,128)(2,1)} %maximum_bitcast_fusion.1), calls=%async_computation.6 | async-start | bytes 196608 | tf_op jit(solution)/shard_map/all_to_all | solution.py:474

commit v2 on v1

v2 whole, which is shorter than its diff:
```python
import functools
import math

import jax
import jax.numpy as jnp
from jax import lax
from jax.experimental import pallas as pl
from jax.experimental.pallas import tpu as pltpu
from jax.sharding import PartitionSpec as P

LANES = 128
TILE = 16
VMEM_LIMIT = 56 * 1024 * 1024


def round_up(value, unit):
    return -(-value // unit) * unit


def fourier_kernel(coarse_cos_ref, coarse_sin_ref, fine_cos_ref, fine_sin_ref, out_ref):
    lon_count = out_ref.shape[1]
    fine_cos, fine_sin = fine_cos_ref[...], fine_sin_ref[...]
    for index in range(-(-lon_count // LANES)):
        width = min(LANES, lon_count - index * LANES)
        coarse_cos = coarse_cos_ref[:, index : index + 1]
        coarse_sin = coarse_sin_ref[:, index : index + 1]
        values = (coarse_cos * fine_cos - coarse_sin * fine_sin).astype(jnp.bfloat16)
        out_ref[:, index * LANES : index * LANES + width] = values[:, :width]


def fourier_rows(waves, lon_count):
    blocks, slots = waves.shape
    rows = blocks * 2 * slots

    def parts(step):
        lons = jnp.arange(LANES, dtype=jnp.int32) * step
        phase = waves[:, :, None] * lons % lon_count
        angle = phase.astype(jnp.float32) * (2.0 * math.pi / lon_count)
        return jnp.cos(angle), jnp.sin(angle)

    def both(first, second):
        return jnp.stack([first, second], axis=1).reshape(rows, LANES)

    coarse_cos, coarse_sin = parts(LANES)
    fine_cos, fine_sin = parts(1)
    return pl.pallas_call(
        fourier_kernel,
        out_shape=jax.ShapeDtypeStruct((rows, lon_count), jnp.bfloat16),
        compiler_params=pltpu.CompilerParams(vmem_limit_bytes=VMEM_LIMIT),
        cost_estimate=pl.CostEstimate(
            flops=3 * rows * lon_count, bytes_accessed=2 * rows * lon_count, transcendentals=0
        ),
    )(
        both(coarse_cos, -coarse_sin),
        both(coarse_sin, coarse_cos),
        both(fine_cos, fine_cos),
        both(fine_sin, fine_sin),
    )


def table_kernel(steps, lane_tiles, top, low_ref, first_ref, second_ref, cos_ref, weight_ref, out_ref, rows_ref, scale_ref):
    tiles = range(lane_tiles)
    low = low_ref[...]
    high = top - low
    low_next = low + 1.0
    lat_count = out_ref.shape[2]
    pairs = out_ref.shape[0]

    def lanes(ref, tile):
        return ref[:, tile * LANES : (tile + 1) * LANES]

    cosines = [lanes(cos_ref, t) for t in tiles]
    weights = [lanes(weight_ref, t) for t in tiles]
    second = [lanes(second_ref, t) for t in tiles]
    for t in tiles:
        half = jnp.exp(0.5 * second[t])
        scale_ref[2, :, t * LANES : (t + 1) * LANES] = half * weights[t]
        scale_ref[3, :, t * LANES : (t + 1) * LANES] = half

    def block(index, carry):
        current, lagged, scale, last_inverse = carry
        for t in tiles:
            largest = jnp.maximum(jnp.maximum(jnp.abs(current[t]), jnp.abs(lagged[t])), 1.0)
            current[t] = current[t] / largest
            lagged[t] = lagged[t] / largest
            scale[t] = scale[t] + jnp.log(largest)
            half = jnp.exp(0.5 * scale[t])
            scale_ref[0, :, t * LANES : (t + 1) * LANES] = half * weights[t]
            scale_ref[1, :, t * LANES : (t + 1) * LANES] = half
        begin = (index * TILE).astype(jnp.float32)
        for step in range(TILE):
            row = begin + float(step)
            after = low < row
            above = row - jnp.where(after, low_next, 0.0)
            order = jnp.where(after, low, high)
            degree = above + order
            spread = above * (degree + order)
            square = 4.0 * degree * degree - 1.0
            root = lax.rsqrt(jnp.maximum(square * spread, 1.0))
            factor = square * root
            inverse = spread * root
            fresh = above == 0.0
            for t in tiles:
                advanced = factor * (cosines[t] * current[t] - last_inverse * lagged[t])
                lagged[t] = current[t]
                current[t] = jnp.where(fresh, 1.0, advanced)
                rows_ref[t, pl.ds(step, pairs, stride=TILE), :] = current[t]
            last_inverse = inverse
        renewed = (low_next >= begin) & (low_next < begin + float(TILE))
        for t in tiles:
            scale[t] = jnp.where(renewed, second[t], scale[t])
        row_index = lax.broadcasted_iota(jnp.int32, (TILE, LANES), 0).astype(jnp.float32) + begin
        for pair in range(pairs):
            mark = low[pair : pair + 1, :]
            before = (row_index <= mark) | (mark + 1.0 < begin)
            for t in tiles:
                span = slice(t * LANES, min((t + 1) * LANES, lat_count))
                width = span.stop - span.start
                here = slice(t * LANES, (t + 1) * LANES)
                values = rows_ref[t, pair * TILE : (pair + 1) * TILE, :]
                one = jnp.where(before, scale_ref[0, pair : pair + 1, here], scale_ref[2, pair : pair + 1, here])
                two = jnp.where(before, scale_ref[1, pair : pair + 1, here], scale_ref[3, pair : pair + 1, here])
                values = (values * one * two).astype(jnp.bfloat16)
                out_ref[pair, pl.ds(pl.multiple_of(index * TILE, TILE), TILE), span] = values[:, :width]
        return current, lagged, scale, last_inverse

    zeros = jnp.zeros((pairs, LANES), jnp.float32)
    start = (
        [zeros for _ in tiles],
        [zeros for _ in tiles],
        [lanes(first_ref, t) for t in tiles],
        zeros,
    )
    lax.fori_loop(0, steps // TILE, block, start)


def packed_table(low_waves, lats, lat_count, degree_count, steps):
    pair_count = low_waves.shape[0]
    lat_half = lats.shape[0]
    lane_tiles = -(-lat_half // LANES)
    width = lane_tiles * LANES
    top = float(degree_count - 1)
    index = jnp.pad(lats, (0, width - lat_half), mode="edge")
    colatitude = (index.astype(jnp.float32) + 0.5) * (math.pi / lat_count)
    sines = jnp.sin(colatitude)
    log_sines = jnp.log(sines)
    low = low_waves.astype(jnp.float32)

    def log_start(order):
        base = 0.5 * (
            jnp.log(order + 0.5)
            + jax.scipy.special.gammaln(order + 0.5)
            - jax.scipy.special.gammaln(order + 1.0)
            - 0.5 * math.log(math.pi)
        )
        return base[:, None] + order[:, None] * log_sines[None, :]

    def spread(row):
        return jnp.broadcast_to(row[None, :], (pair_count, width))

    return pl.pallas_call(
        functools.partial(table_kernel, steps, lane_tiles, top),
        out_shape=jax.ShapeDtypeStruct((pair_count, steps, lat_half), jnp.bfloat16),
        scratch_shapes=[
            pltpu.VMEM((lane_tiles, pair_count * TILE, LANES), jnp.float32),
            pltpu.VMEM((4, pair_count, width), jnp.float32),
        ],
        compiler_params=pltpu.CompilerParams(vmem_limit_bytes=VMEM_LIMIT),
        cost_estimate=pl.CostEstimate(
            flops=pair_count * steps * width * 60, bytes_accessed=pair_count * steps * width * 2, transcendentals=0
        ),
    )(
        jnp.broadcast_to(low[:, None], (pair_count, LANES)),
        log_start(top - low),
        log_start(low),
        spread(jnp.cos(colatitude)),
        spread(sines * (math.pi / lat_count)),
    )


def gather_slots(in_refs, flat_ref, slot_ref):
    lats, rows, days = in_refs[0].shape
    lat_half = len(in_refs) * lats
    for part in range(2):
        for source, in_ref in enumerate(in_refs):
            values = in_ref[:, part * TILE : (part + 1) * TILE, :].astype(jnp.float32)
            flat_ref[pl.ds(source * lats * TILE, lats * TILE), :] = values.reshape(lats * TILE, days)
        for slot in range(TILE):
            column = flat_ref[pl.ds(slot, lat_half, stride=TILE), :]
            slot_ref[slot, :, part * days : (part + 1) * days] = column.astype(jnp.bfloat16)


def pair_sum(pair, low, table_ref, slot_ref):
    table = table_ref[pair]
    high_sum = jnp.dot(table, slot_ref[2 * pair], preferred_element_type=jnp.float32)
    low_sum = jnp.dot(table, slot_ref[2 * pair + 1], preferred_element_type=jnp.float32)
    row = lax.broadcasted_iota(jnp.int32, high_sum.shape, 0)
    return jnp.where(row <= low, high_sum, low_sum)


def partial_kernel(low_ref, table_ref, *rest):
    out_ref, flat_ref, slot_ref = rest[-3:]
    gather_slots(rest[:-3], flat_ref, slot_ref)

    def one(pair, carry):
        out_ref[pair] = pair_sum(pair, low_ref[pair], table_ref, slot_ref).astype(jnp.bfloat16)
        return carry

    lax.fori_loop(0, TILE // 2, one, 0)


def finish_kernel(sources, low_ref, wave_ref, shift_ref, table_ref, other_ref, own_ref, season_ref, *rest):
    out_ref, misc_ref, flat_ref, slot_ref, turned_ref = rest[-5:]
    steps = table_ref.shape[1]
    days = out_ref.shape[0]
    degrees = out_ref.shape[3]
    lane_tiles = degrees // LANES
    gather_slots(rest[:sources], flat_ref, slot_ref)
    lane = lax.broadcasted_iota(jnp.int32, (steps, LANES), 1)
    turn = (
        lax.broadcasted_iota(jnp.int32, (days, days), 0) == lax.broadcasted_iota(jnp.int32, (days, days), 1)
    ).astype(jnp.bfloat16)
    pick_row = lax.broadcasted_iota(jnp.int32, (8, LANES), 0)
    pick_lane = lax.broadcasted_iota(jnp.int32, (8, LANES), 1)
    wanted = jnp.where(pick_row == 1, 2, jnp.where(pick_row == 2, LANES - 1, 0))
    wanted = jnp.where(pick_row > 2, jnp.where(pick_row == 3, 1, pick_row - 1), wanted)
    pick = ((pick_lane == wanted) & (pick_row < 6)).astype(jnp.bfloat16)
    row = lax.broadcasted_iota(jnp.int32, (steps, degrees), 0)
    degree = lax.broadcasted_iota(jnp.int32, (steps, degrees), 1)
    transposed = (((1,), (1,)), ((), ()))

    def one(pair, carry):
        own = pair_sum(pair, low_ref[pair], table_ref, slot_ref)
        total = own + other_ref[pair].astype(jnp.float32)
        places = []
        own_rows = jnp.zeros((steps, 8), jnp.float32)
        for position in range(2):
            slot = 2 * pair + position
            chosen = (row - degree == shift_ref[slot]) & (degree >= wave_ref[slot])
            places.append(chosen.astype(jnp.bfloat16))
            own_rows = own_rows + lax.dot_general(
                places[position], own_ref[slot], transposed, preferred_element_type=jnp.float32
            )
        ar = own_rows[:, 0:1] + own_rows[:, 1:2]
        half = own_rows[:, 2:3] + own_rows[:, 3:4]
        turned = []
        parts = []
        sum_coef = jnp.zeros((steps, LANES), jnp.float32)
        sum_var = jnp.zeros((steps, LANES), jnp.float32)
        for part in range(2):
            spectral = total[:, part * days : (part + 1) * days]
            parts.append(spectral)
            previous = jnp.where(lane == 0, 0.0, pltpu.roll(spectral, 1, 1))
            residual = spectral - ar * previous
            scaled = residual * season_ref[0:1, :]
            innovation = (scaled * half).astype(jnp.bfloat16)
            turned.append(
                lax.dot_general(turn, innovation, transposed, preferred_element_type=jnp.float32)
            )
            weighted = residual * season_ref[1:2, :]
            sum_coef = sum_coef + weighted * previous
            sum_var = sum_var + weighted * residual
        sum_coef = jnp.sum(sum_coef, axis=1, keepdims=True)
        sum_var = jnp.sum(sum_var, axis=1, keepdims=True)
        misc = jnp.where(
            (lane == 0) | (lane == LANES - 1),
            parts[0],
            jnp.where(lane < 3, pltpu.roll(parts[1], 2, 1), jnp.where(lane == 3, sum_coef, sum_var)),
        )
        misc_high = misc.astype(jnp.bfloat16)
        misc_low = (misc - misc_high.astype(jnp.float32)).astype(jnp.bfloat16)
        for piece in (misc_high, misc_low):
            turned.append(lax.dot_general(pick, piece, transposed, preferred_element_type=jnp.float32))
        stacked = jnp.concatenate(turned, axis=0).astype(jnp.bfloat16)
        for position in range(2):
            slot = 2 * pair + position
            placed = jnp.dot(stacked, places[position], preferred_element_type=jnp.float32)
            for part in range(2):
                for t in range(lane_tiles):
                    turned_ref[part, t, pl.ds(slot, days, stride=TILE), :] = placed[
                        part * days : (part + 1) * days, t * LANES : (t + 1) * LANES
                    ]
            misc_ref[slot] = placed[2 * days : 2 * days + 8] + placed[2 * days + 8 : 2 * days + 16]
        return carry

    lax.fori_loop(0, TILE // 2, one, 0)

    def write(day, carry):
        for part in range(2):
            for t in range(lane_tiles):
                values = turned_ref[part, t, pl.ds(pl.multiple_of(day * TILE, TILE), TILE), :]
                out_ref[day, part, :, t * LANES : (t + 1) * LANES] = values.astype(jnp.bfloat16)
        return carry

    lax.fori_loop(0, days, write, 0)


def leading(shape, chunk):
    return pl.BlockSpec(shape, lambda i: (chunk,) + (0,) * (len(shape) - 1))


def partial_sums(chunk, low, blocks, table):
    lats, rows, days = blocks[0].shape
    steps, lat_half = table.shape[1:]
    pairs = TILE // 2
    return pl.pallas_call(
        partial_kernel,
        grid=(1,),
        in_specs=[
            pl.BlockSpec(memory_space=pltpu.SMEM),
            leading((pairs, steps, lat_half), chunk),
        ]
        + [leading(block.shape, 0) for block in blocks],
        out_specs=leading((pairs, steps, 2 * days), 0),
        out_shape=jax.ShapeDtypeStruct((pairs, steps, 2 * days), jnp.bfloat16),
        scratch_shapes=[
            pltpu.VMEM((lat_half * TILE, days), jnp.float32),
            pltpu.VMEM((TILE, lat_half, 2 * days), jnp.bfloat16),
        ],
        compiler_params=pltpu.CompilerParams(vmem_limit_bytes=VMEM_LIMIT),
        cost_estimate=pl.CostEstimate(
            flops=6 * TILE * steps * lat_half * 2 * days, bytes_accessed=8 * 1024 * 1024, transcendentals=0
        ),
    )(low, table, *blocks)


def finish(chunk, low, waves, shifts, blocks, table, other, own, season, held, slot_total):
    lats, rows, days = blocks[0].shape
    steps, lat_half = table.shape[1:]
    pairs = TILE // 2
    degrees = own.shape[2]
    smem = pl.BlockSpec(memory_space=pltpu.SMEM)
    operands = [low, waves, shifts, table, other, own, season, *blocks]
    in_specs = [
        smem,
        smem,
        smem,
        leading((pairs, steps, lat_half), chunk),
        leading((pairs, steps, 2 * days), 0),
        leading((TILE, 8, degrees), chunk),
        leading((8, LANES), 0),
    ] + [leading(block.shape, 0) for block in blocks]
    aliases = {}
    if held is not None:
        operands.append(held)
        in_specs.append(pl.BlockSpec(memory_space=pl.ANY))
        aliases = {len(operands) - 1: 0}
    return pl.pallas_call(
        functools.partial(finish_kernel, len(blocks)),
        grid=(1,),
        in_specs=in_specs,
        out_specs=[
            pl.BlockSpec((days, 2, TILE, degrees), lambda i: (0, 0, chunk, 0)),
            leading((TILE, 8, degrees), 0),
        ],
        out_shape=[
            jax.ShapeDtypeStruct((days, 2, slot_total, degrees), jnp.bfloat16),
            jax.ShapeDtypeStruct((TILE, 8, degrees), jnp.float32),
        ],
        input_output_aliases=aliases,
        scratch_shapes=[
            pltpu.VMEM((lat_half * TILE, days), jnp.float32),
            pltpu.VMEM((TILE, lat_half, 2 * days), jnp.bfloat16),
            pltpu.VMEM((2, degrees // LANES, days * TILE, LANES), jnp.float32),
        ],
        compiler_params=pltpu.CompilerParams(vmem_limit_bytes=VMEM_LIMIT),
        cost_estimate=pl.CostEstimate(
            flops=12 * TILE * steps * lat_half * 2 * days, bytes_accessed=12 * 1024 * 1024, transcendentals=0
        ),
    )(*operands)


def split_rows(values):
    high = lax.reduce_precision(values, 8, 7)
    return high.astype(jnp.bfloat16), (values - high).astype(jnp.bfloat16)


def after(values, waited):
    return lax.optimization_barrier((values, waited))[0]


def per_device(fields, wave_table, day_of_year, ar_coef, log_var):
    band_count = lax.axis_size("band")
    time_count = lax.axis_size("tm")
    band = lax.axis_index("band")
    slot_count, degree_count = ar_coef.shape
    day_count, lat_local, lon_count = fields.shape
    lat_count = lat_local * band_count
    group = band_count // 2
    steps = round_up(degree_count + 1, TILE)
    total_days = day_count * time_count
    slot_pad = round_up(slot_count, TILE)
    chunks = slot_pad // TILE
    pairs = slot_pad // 2
    half_index = band // group
    rank = band % group
    mirror = [(i, (i + group) % band_count) for i in range(band_count)]
    peers = [rank ^ k for k in range(group)]

    waves = wave_table.reshape(2, group, slot_count // 2, 2)
    high_low = jnp.stack([waves.max(-1), waves.min(-1)], axis=-1)
    high_low = jnp.pad(high_low, ((0, 0), (0, 0), (0, pairs - slot_count // 2), (0, 0)))
    ordered = high_low.reshape(2, group, slot_pad)
    present = jnp.arange(slot_pad) < slot_count

    def by_peer(side):
        table = lax.dynamic_index_in_dim(ordered, side, 0, keepdims=False)
        return jnp.stack([lax.dynamic_index_in_dim(table, peer, 0, keepdims=False) for peer in peers])

    own_waves, far_waves = by_peer(half_index), by_peer(1 - half_index)
    own_low, far_low = own_waves[0, 1::2], far_waves[0, 1::2]
    lats = jnp.concatenate(
        [(half_index * group + peer) * lat_local + jnp.arange(lat_local, dtype=jnp.int32) for peer in peers]
    )

    def transform(source, waves_of, first, count):
        picked = waves_of[:, first * TILE : (first + count) * TILE].reshape(group * count, TILE)
        table = fourier_rows(picked, lon_count)
        if slot_pad != slot_count:
            mask = present[first * TILE : (first + count) * TILE].reshape(count, 1, TILE)
            mask = jnp.broadcast_to(mask, (group, count, 2, TILE)).reshape(-1, 1)
            table = table * mask.astype(jnp.bfloat16)
        coeffs = jnp.einsum("djk,qk->jqd", source, table, preferred_element_type=jnp.float32)
        coeffs = coeffs.astype(jnp.bfloat16).reshape(lat_local, group, count, 2 * TILE, day_count)
        return [[coeffs[:, peer, i] for peer in range(group)] for i in range(count)]

    def exchange(blocks):
        moved = [
            lax.ppermute(blocks[k], "band", [(i, i ^ k) for i in range(band_count)]) for k in range(1, group)
        ]
        return [blocks[0]] + moved

    far_blocks = transform(fields, far_waves, 0, 1)
    arrived = [exchange(far_blocks[0])]
    if chunks > 1:
        far_blocks = far_blocks + transform(after(fields, far_blocks[0][0]), far_waves, 1, chunks - 1)
    far_table = packed_table(after(far_low, far_blocks[-1][0]), lats, lat_count, degree_count, steps)

    def queue(blocks):
        if len(arrived) > 1:
            blocks = after(blocks, arrived[-2][1])
        arrived.append(exchange(blocks))

    for chunk in range(1, chunks):
        queue(far_blocks[chunk])

    others = []

    def send_sums(chunk):
        low = far_low[chunk * TILE // 2 : (chunk + 1) * TILE // 2]
        sums = partial_sums(chunk, low, arrived[chunk], far_table)
        others.append(lax.ppermute(sums, "band", mirror))
        return sums

    first_sums = send_sums(0)
    own_blocks = transform(after(fields, first_sums), own_waves, 0, chunks)
    own_table = packed_table(after(own_low, own_blocks[0][0]), lats, lat_count, degree_count, steps)
    for chunk in range(chunks):
        queue(own_blocks[chunk])
        if chunk + 1 < chunks:
            send_sums(chunk + 1)

    slot_waves = lax.dynamic_slice_in_dim(wave_table, band * slot_count, slot_count)
    pad_slots = (0, slot_pad - slot_count)
    kernel_waves = jnp.pad(slot_waves, pad_slots)
    is_low = kernel_waves == jnp.repeat(own_low, 2)
    shifts = jnp.where(is_low, 1, -kernel_waves)
    own_rows = jnp.stack([*split_rows(ar_coef), *split_rows(jnp.exp(-0.5 * log_var))], axis=1)
    own_rows = jnp.pad(own_rows, (pad_slots, (0, 4), (0, 0)))
    season = 1.0 + 0.5 * jnp.cos(day_of_year.astype(jnp.float32) * (2.0 * math.pi / 365.0))
    later = (jnp.arange(day_count) > 0).astype(jnp.float32)
    season_rows = jnp.pad(jnp.stack([lax.rsqrt(season), later / season]), ((0, 6), (0, 0)))

    innovation = None
    misc = []
    for chunk in range(chunks):
        low = own_low[chunk * TILE // 2 : (chunk + 1) * TILE // 2]
        span = slice(chunk * TILE, (chunk + 1) * TILE)
        innovation, rows = finish(
            chunk, low, kernel_waves[span], shifts[span], arrived[chunks + chunk], own_table, others[chunk],
            own_rows, season_rows, innovation, slot_pad,
        )
        misc.append(rows)
    innovation = innovation[:, :, :slot_count]
    misc = jnp.concatenate(misc, axis=0)[:slot_count, :6]

    degree_list = jnp.arange(degree_count, dtype=jnp.int32)
    valid_mask = (degree_list[None, :] >= slot_waves[:, None]).astype(jnp.float32)
    edges = misc.transpose(1, 0, 2)
    route = [(i, i + 1) for i in range(time_count - 1)]
    carried = lax.ppermute(edges[2:4].astype(jnp.bfloat16), "tm", route).astype(jnp.float32)
    scale = jnp.exp(-0.5 * log_var) * lax.rsqrt(season[0]) * valid_mask
    opening = ((edges[0:2] - ar_coef[None] * carried) * scale[None]).astype(jnp.bfloat16)
    innovation = lax.dynamic_update_slice_in_dim(innovation, opening[None], 0, 0)

    column_width = degree_count // time_count
    place = lax.axis_index("tm")
    columns = [misc[:, :, i * column_width : (i + 1) * column_width] for i in range(time_count)]
    moved = lax.all_to_all(jnp.stack(columns).astype(jnp.bfloat16), "tm", 0, 0, tiled=True).astype(jnp.float32)

    def own_columns(values):
        return lax.dynamic_slice_in_dim(values, place * column_width, column_width, 1)

    local_ar, local_var = own_columns(ar_coef), jnp.exp(-own_columns(log_var))
    first_days = day_of_year[0] + (jnp.arange(time_count, dtype=jnp.int32) - place) * day_count
    first_days = (first_days % 365).astype(jnp.float32)
    openness = 1.0 / (1.0 + 0.5 * jnp.cos(first_days * (2.0 * math.pi / 365.0)))
    first = moved[:, :, 0:2]
    before = jnp.concatenate([jnp.zeros_like(moved[:1, :, 2:4]), moved[:-1, :, 2:4]], axis=0)
    residual = first - local_ar[None, :, None] * before
    weighted = residual * openness[:, None, None, None]
    sum_coef = jnp.sum(moved[:, :, 4], axis=0) + jnp.sum(weighted * before, axis=(0, 2))
    sum_var = jnp.sum(moved[:, :, 5], axis=0) + jnp.sum(weighted * residual, axis=(0, 2))
    local_mask = own_columns(valid_mask)
    grad_coef = -local_mask * local_var * sum_coef / (2.0 * total_days)
    grad_var = local_mask * (total_days - 0.5 * local_var * sum_var) / (2.0 * total_days)
    return innovation, grad_coef, grad_var


def solution(mesh):
    in_specs = (P("tm", "band", None), P(), P("tm"), P("band", None), P("band", None))
    out_specs = (P("tm", None, "band", None), P("band", "tm"), P("band", "tm"))
    return jax.shard_map(
        per_device, mesh=mesh, in_specs=in_specs, out_specs=out_specs, check_vma=False
    )
```

time: 632 us -> 398 us (0.63)
  local copies, waits for them, and re-layouts: 215 us -> 24.2 us
  waiting for transfers between devices: 168 us -> 116 us
  Pallas kernels: 127 us -> 151 us
  starting transfers between devices: 41.2 us -> 31.6 us
    gather x5 -> x0, local copies, waits for them, and re-layouts: 146 us -> none  [pack_rows(): jnp.take_along_axis(values.reshape(values.shape[0], 2 * degrees), source,...]
    all_to_all x7 -> x1, waiting for transfers between devices: 91.2 us -> 5.59 us  [per_device(): lax.all_to_all(jnp.stack(columns).astype(jnp.bfloat16), 'tm', 0, 0, tiled...]
    ppermute x4 -> x22, waiting for transfers between devices: 76.5 us -> 110 us  [the longest x18 110 us: exchange(): lax.ppermute(blocks[k], 'band', [(i, i ^ k) for i in range(band_count)])]
    all_to_all x7 -> x1, starting transfers between devices: 34.3 us -> 3.49 us  [per_device(): lax.all_to_all(jnp.stack(columns).astype(jnp.bfloat16), 'tm', 0, 0, tiled...]
    pallas_call x4 -> x8, Pallas kernels: 97.1 us -> 121 us  [the longest x3 75.6 us: finish(): pl.pallas_call(functools.partial(finish_kernel, len(blocks)), grid=(1,),...]
    ppermute x4 -> x22, starting transfers between devices: 6.97 us -> 28.1 us  [the longest x18 20.6 us: exchange(): lax.ppermute(blocks[k], 'band', [(i, i ^ k) for i in range(band_count)])]
    slice x13 -> x7, local copies, waits for them, and re-layouts: 15.3 us -> 1.63 us  [the longest x1 0.66 us: send_sums(): low = far_low[chunk * TILE // 2:(chunk + 1) * TILE // 2]]
    unnamed x39 -> x24, local copies, waits for them, and re-layouts: 16 us -> 4.03 us
  transfers between devices with their start and end apart: 11 -> 23, of which waited for: 7 -> 7; matrix products, arithmetic and copies ran while one was open for 41% -> 17% of each run, Pallas kernels for 17% -> 32%
where the time goes in v2:
time: 398 us; the launch traced here: 390 us
  Pallas kernels  151 us (38%)
  waiting for transfers between devices  116 us (29%)
  matrix products  52 us (13%)
  starting transfers between devices  31.6 us (8%)
  local copies, waits for them, and re-layouts  24.2 us (6%)
  other arithmetic  14.2 us (4%)
    ppermute x18, waiting for transfers between devices, exchange(): lax.ppermute(blocks[k], 'band', [(i, i ^ k) for i in range(band_count)])  110 us
    pallas_call x3, Pallas kernels, finish(): pl.pallas_call(functools.partial(finish_kernel, len(blocks)), grid=(1,),...  75.6 us
    dot_general x3, matrix products, transform(): jnp.einsum('djk,qk->jqd', source, table, preferred_element_type=jnp.float32)  52 us
    pallas_call x2, Pallas kernels, packed_table(): pl.pallas_call(functools.partial(table_kernel, steps, lane_tiles, top), o...  37.1 us
    pallas_call x3, Pallas kernels, partial_sums(): pl.pallas_call(partial_kernel, grid=(1,), in_specs=[pl.BlockSpec(memory_s...  29.5 us
    ppermute x18, starting transfers between devices, exchange(): lax.ppermute(blocks[k], 'band', [(i, i ^ k) for i in range(band_count)])  20.6 us
    squeeze x3, local copies, waits for them, and re-layouts, transform(): return [[coeffs[:, peer, i] for peer in range(group)] for i in range(count)]  9.52 us
    pallas_call x3, Pallas kernels, fourier_rows(): pl.pallas_call(fourier_kernel, out_shape=jax.ShapeDtypeStruct((rows, lon_...  8.57 us
  transfers between devices with their start and end apart: 23, of which 7 were waited for; matrix products, arithmetic and copies ran while one was open for 17% of the time, Pallas kernels for 32%

profile of v2, /device:TPU:0, one launch (start us, length us, event | category | flops | bytes accessed | tf_op | source)
XLA Modules:
  0.0 390.3 jit_solution(18250974779056290737)
XLA Ops:
  0.7 0.8 reshape.407
  2.7 0.6 pad_maximum_fusion.11
  4.0 0.7 pad_maximum_fusion.10
  4.7 2.2 shard_map.78
  6.8 15.0 %convolution_convert_fusion.2 = bf16[128,128,88]{1,0,2:T(8,128)(2,1)S(1)} fusion(bf16[128,88,1440]{0,2,1:T(8,128)(2,1)} %param.5, bf16[128,1440]{1,0:T(8,128)(2,1)} %shard_map.78), kind=kOutput, calls=%fused_computation.2 | convolution fusion | flops 4153802752 | bytes 35692544 | tf_op jit(solution)/shard_map/djk,qk->jqd/dot_general | solution.py:423
  21.9 1.6 slice_bitcast_fusion.19
  23.5 3.0 collective-permute-start
  26.5 1.6 collective-permute-start.1
  28.8 0.7 pad_maximum_fusion.7
  29.5 0.7 pad_maximum_fusion.8
  30.2 0.7 pad_maximum_fusion.6
  30.9 2.9 shard_map.77
  33.8 15.6 %convolution_convert_fusion.1 = bf16[256,128,88]{1,0,2:T(8,128)(2,1)S(1)} fusion(bf16[128,88,1440]{0,2,1:T(8,128)(2,1)} %param.5, bf16[256,1440]{1,0:T(8,128)(2,1)} %shard_map.77), kind=kOutput, calls=%fused_computation.1 | convolution fusion | flops 8307605504 | bytes 38944768 | tf_op jit(solution)/shard_map/djk,qk->jqd/dot_general | solution.py:423
  49.4 2.5 slice_bitcast_fusion.4
  51.9 1.9 collective-permute-start.7
  53.8 1.6 collective-permute-start.12
  55.8 0.7 slice_bitcast_fusion.29
  57.2 0.6 reshape.424
  58.1 0.9 fusion.25
  59.0 0.7 pad_maximum_fusion.3
  59.7 0.7 pad_maximum_fusion.4
  60.5 0.8 compare_select_fusion.16
  61.7 0.8 pad_maximum_fusion.2
  62.5 1.1 fusion.9.own_ref
  63.7 0.7 multiply_add_fusion.2
  65.0 3.5 shard_map.76
  68.5 0.7 broadcast_in_dim.20.low_ref
  70.4 18.6 %shard_map.79.table_ref = bf16[24,400,352]{2,1,0:T(8,128)(2,1)} custom-call(f32[24,128]{1,0:T(8,128)} %broadcast_in_dim.20.low_ref, f32[24,384]{1,0:T(8,128)} %get-tuple-element.133.first_ref, f32[24,384]{1,0:T(8,128)} %get-tuple-element.132.second_ref, f32[24,384]{1,0:T(8,128)} %broadcast_in_dim.21.cos_ref, f32[24,384]{1,0:T(8,128)} %broadcast_in_dim.22.weight_ref), custom_call_target="tpu_custom_call" | custom-call | flops 221184000 | bytes 7372800 | tf_op jit(solution)/shard_map/pallas_call | solution.py:161
  89.0 0.7 slice_bitcast_fusion.30
  90.5 9.9 %shard_map.80 = bf16[8,400,256]{2,1,0:T(8,128)(2,1)} custom-call(s32[8]{0:T(128)} %get-tuple-element.147.low_ref, bf16[24,400,352]{2,1,0:T(8,128)(2,1)} %shard_map.79.table_ref, bf16[88,32,128]{2,1,0:T(8,128)(2,1)} %get-tuple-element.96.rest_0_, bf16[88,32,128]{2,1,0:T(8,128)(2,1)} %collective-permute-done.rest_1_, ...), custom_call_target="tpu_custom_call" | custom-call | flops 3460300800 | bytes 8388608 | tf_op jit(solution)/shard_map/pallas_call | solution.py:306
  100.3 3.0 collective-permute-start.18
  103.3 1.5 collective-permute-start.3
  104.8 21.4 %convolution_convert_fusion = bf16[384,128,88]{1,0,2:T(8,128)(2,1)} fusion(bf16[128,88,1440]{0,2,1:T(8,128)(2,1)} %param.5, bf16[384,1440]{1,0:T(8,128)(2,1)S(1)} %copy-done), kind=kOutput, calls=%fused_computation | convolution fusion | flops 12461408256 | bytes 42196992 | tf_op jit(solution)/shard_map/djk,qk->jqd/dot_general | solution.py:423
  126.2 1.6 collective-permute-start.4
  128.2 5.3 %slice_bitcast_fusion = (bf16[88,32,128]{2,1,0:T(8,128)(2,1)S(1)}, bf16[88,32,128]{2,1,0:T(8,128)(2,1)S(1)}, bf16[88,32,128]{2,1,0:T(8,128)(2,1)S(1)}, bf16[88,3...) fusion(bf16[88,4,3,32,128]{4,3,2,1,0:T(8,128)(2,1)} %bitcast.185), kind=kLoop, calls=%fused_computation.5 | loop fusion | bytes 17301504 | tf_op jit(solution)/shard_map/squeeze | solution.py:425
  133.6 1.6 collective-permute-start.8
  135.1 9.9 %shard_map.83 = bf16[8,400,256]{2,1,0:T(8,128)(2,1)} custom-call(s32[8]{0:T(128)} %get-tuple-element.145.low_ref, bf16[24,400,352]{2,1,0:T(8,128)(2,1)} %shard_map.79.table_ref, bf16[88,32,128]{2,1,0:T(8,128)(2,1)} %get-tuple-element.87.rest_0_, bf16[88,32,128]{2,1,0:T(8,128)(2,1)} %collective-permute-done.7.rest_1_, ...), custom_call_target="tpu_custom_call" | custom-call | flops 3460300800 | bytes 8388608 | tf_op jit(solution)/shard_map/pallas_call | solution.py:306
  145.5 29.4 %collective-permute-done.4.rest_2_ = bf16[88,32,128]{2,1,0:T(8,128)(2,1)} collective-permute-done((bf16[88,32,128]{2,1,0:T(8,128)(2,1)}, bf16[88,32,128]{2,1,0:T(8,128)(2,1)}, u32[]{:S(2)}, u32[]{:S(2)}) %collective-permute-start.4) | collective-permute-done | bytes 720928 | tf_op jit(solution)/shard_map/ppermute | solution.py:429
  174.9 17.0 %collective-permute-done.5.rest_3_ = bf16[88,32,128]{2,1,0:T(8,128)(2,1)} collective-permute-done((bf16[88,32,128]{2,1,0:T(8,128)(2,1)S(1)}, bf16[88,32,128]{2,1,0:T(8,128)(2,1)}, u32[]{:S(2)}, u32[]{:S(2)}) %collective-permute-start.5) | collective-permute-done | bytes 720928 | tf_op jit(solution)/shard_map/ppermute | solution.py:429
  192.0 9.8 %shard_map.82 = bf16[8,400,256]{2,1,0:T(8,128)(2,1)} custom-call(s32[8]{0:T(128)} %get-tuple-element.146.low_ref, bf16[24,400,352]{2,1,0:T(8,128)(2,1)} %shard_map.79.table_ref, bf16[88,32,128]{2,1,0:T(8,128)(2,1)} %get-tuple-element.33.rest_0_, bf16[88,32,128]{2,1,0:T(8,128)(2,1)} %collective-permute-done.3.rest_1_, ...), custom_call_target="tpu_custom_call" | custom-call | flops 3460300800 | bytes 8388608 | tf_op jit(solution)/shard_map/pallas_call | solution.py:306
  201.8 2.9 collective-permute-start.6
  204.7 0.7 multiply_add_fusion
  205.4 0.7 broadcast_in_dim.23.low_ref
  206.0 18.5 %shard_map.81.table_ref = bf16[24,400,352]{2,1,0:T(8,128)(2,1)} custom-call(f32[24,128]{1,0:T(8,128)} %broadcast_in_dim.23.low_ref, f32[24,384]{1,0:T(8,128)} %get-tuple-element.128.first_ref, f32[24,384]{1,0:T(8,128)} %get-tuple-element.127.second_ref, f32[24,384]{1,0:T(8,128)} %broadcast_in_dim.21.cos_ref, f32[24,384]{1,0:T(8,128)} %broadcast_in_dim.22.weight_ref), custom_call_target="tpu_custom_call" | custom-call | flops 221184000 | bytes 7372800 | tf_op jit(solution)/shard_map/pallas_call | solution.py:161
  224.5 1.3 collective-permute-start.15
  225.8 24.4 %collective-permute-done.20.rest_3_ = bf16[88,32,128]{2,1,0:T(8,128)(2,1)S(1)} collective-permute-done((bf16[88,32,128]{2,1,0:T(8,128)(2,1)S(1)}, bf16[88,32,128]{2,1,0:T(8,128)(2,1)S(1)}, u32[]{:S(2)}, u32[]{:S(2)}) %collective-permute-start.20) | collective-permute-done | bytes 720928 | tf_op jit(solution)/shard_map/ppermute | solution.py:429
  250.4 3.4 collective-permute-start.17
  253.8 25.4 %shard_map.84 = (bf16[128,2,48,384]{3,2,1,0:T(8,128)(2,1)}, f32[16,8,384]{2,1,0:T(8,128)}) custom-call(s32[8]{0:T(128)} %get-tuple-element.142.low_ref, s32[16]{0:T(128)} %get-tuple-element.158.wave_ref, s32[16]{0:T(128)} %get-tuple-element.136.shift_ref, bf16[24,400,352]{2,1,0:T(8,128)(2,1)} %shard_map.81.table_ref, ...), custom_call_target="tpu_custom_call" | custom-call | flops 6920601600 | bytes 12582912 | tf_op jit(solution)/shard_map/pallas_call | solution.py:348
  279.2 0.9 constant_dynamic-update-slice_fusion.2
  280.2 9.8 %collective-permute-done.16.rest_2_ = bf16[88,32,128]{2,1,0:T(8,128)(2,1)S(1)} collective-permute-done((bf16[88,32,128]{2,1,0:T(8,128)(2,1)S(1)}, bf16[88,32,128]{2,1,0:T(8,128)(2,1)S(1)}, u32[]{:S(2)}, u32[]{:S(2)}) %collective-permute-start.16) | collective-permute-done | bytes 720928 | tf_op jit(solution)/shard_map/ppermute | solution.py:429
  290.0 2.5 collective-permute-start.10
  292.5 29.6 %collective-permute-done.17.rest_3_ = bf16[88,32,128]{2,1,0:T(8,128)(2,1)S(1)} collective-permute-done((bf16[88,32,128]{2,1,0:T(8,128)(2,1)S(1)}, bf16[88,32,128]{2,1,0:T(8,128)(2,1)S(1)}, u32[]{:S(2)}, u32[]{:S(2)}) %collective-permute-start.17) | collective-permute-done | bytes 720928 | tf_op jit(solution)/shard_map/ppermute | solution.py:429
  322.1 0.8 copy-done.8
  323.0 25.2 %shard_map.85 = (bf16[128,2,48,384]{3,2,1,0:T(8,128)(2,1)}, f32[16,8,384]{2,1,0:T(8,128)}) custom-call(s32[8]{0:T(128)} %get-tuple-element.143.low_ref, s32[16]{0:T(128)} %get-tuple-element.157.wave_ref, s32[16]{0:T(128)} %get-tuple-element.137.shift_ref, bf16[24,400,352]{2,1,0:T(8,128)(2,1)} %shard_map.81.table_ref, ...), custom_call_target="tpu_custom_call", output_to_operand_aliasing={{0}: (11, {})} | custom-call | flops 6920601600 | bytes 12582912 | tf_op jit(solution)/shard_map/pallas_call | solution.py:348
  348.1 0.9 constant_dynamic-update-slice_fusion.1
  349.2 0.7 copy-done.5
  350.5 25.1 %shard_map.86 = (bf16[128,2,48,384]{3,2,1,0:T(8,128)(2,1)}, f32[16,8,384]{2,1,0:T(8,128)}) custom-call(s32[8]{0:T(128)} %get-tuple-element.144.low_ref, s32[16]{0:T(128)} %get-tuple-element.156.wave_ref, s32[16]{0:T(128)} %get-tuple-element.138.shift_ref, bf16[24,400,352]{2,1,0:T(8,128)(2,1)} %shard_map.81.table_ref, ...), custom_call_target="tpu_custom_call", output_to_operand_aliasing={{0}: (11, {})} | custom-call | flops 6920601600 | bytes 12582912 | tf_op jit(solution)/shard_map/pallas_call | solution.py:348
  375.6 0.9 constant_dynamic-update-slice_fusion
  376.7 1.3 collective-permute-start.21
  378.3 0.8 copy.113
  379.0 3.5 all-to-all-start
  382.7 0.6 copy_dynamic-update-slice_fusion
  383.3 5.6 %all-to-all-done = bf16[4,48,6,96]{3,1,2,0:T(8,128)(2,1)S(1)} async-done(((bf16[4,48,6,96]{3,1,2,0:T(8,128)(2,1)}), bf16[4,48,6,96]{3,1,2,0:T(8,128)(2,1)S(1)}, u32[]{:S(2)}, u32[]{:S(2)}) %all-to-all-start) | async-done | bytes 221216 | tf_op jit(solution)/shard_map/all_to_all | solution.py:499
  389.1 0.7 fusion.65
  (96 shorter events, 9.7 us)
Async XLA Ops:
  23.5 66.9 %collective-permute-start = (bf16[88,32,128]{2,1,0:T(8,128)(2,1)}, bf16[88,32,128]{2,1,0:T(8,128)(2,1)}, u32[]{:S(2)}, u32[]{:S(2)}) collective-permute-start(bf16[88,32,128]{2,1,0:T(8,128)(2,1)} %get-tuple-element.95), channel_id=1, source_target_pairs={{0,4},{4,0},{8,12},{12,8},{16,20},{20,16},{24,28},{28,24},{1,5},{5... | collective-permute-start | bytes 2162696 | tf_op jit(solution)/shard_map/ppermute | solution.py:429
  26.5 64.0 %collective-permute-start.1 = (bf16[88,32,128]{2,1,0:T(8,128)(2,1)}, bf16[88,32,128]{2,1,0:T(8,128)(2,1)}, u32[]{:S(2)}, u32[]{:S(2)}) collective-permute-start(bf16[88,32,128]{2,1,0:T(8,128)(2,1)} %get-tuple-element.94), channel_id=1, source_target_pairs={{0,8},{4,12},{8,0},{12,4},{16,24},{20,28},{24,16},{28,20},{1,9},{5... | collective-permute-start | bytes 2162696 | tf_op jit(solution)/shard_map/ppermute | solution.py:429
  28.1 62.4 %collective-permute-start.2 = (bf16[88,32,128]{2,1,0:T(8,128)(2,1)S(1)}, bf16[88,32,128]{2,1,0:T(8,128)(2,1)}, u32[]{:S(2)}, u32[]{:S(2)}) collective-permute-start(bf16[88,32,128]{2,1,0:T(8,128)(2,1)S(1)} %get-tuple-element.93), channel_id=1, source_target_pairs={{0,12},{4,8},{8,4},{12,0},{16,28},{20,24},{24,20},{28,16},{1,13},{... | collective-permute-start | bytes 2162696 | tf_op jit(solution)/shard_map/ppermute | solution.py:429
  49.3 11.0 %copy-start.10 = (s32[128]{0:T(128)S(1)}, s32[128]{0:T(128)}, u32[]{:S(2)}) copy-start(s32[128]{0:T(128)} %param.7) | copy-start | bytes 1540
  49.4 11.9 %copy-start.2 = (f32[48,384]{1,0:T(8,128)S(1)}, f32[48,384]{1,0:T(8,128)}, u32[]{:S(2)}) copy-start(f32[48,384]{1,0:T(8,128)} %param.9) | copy-start | bytes 221188
  49.4 12.1 %copy-start.1 = (f32[48,384]{1,0:T(8,128)S(1)}, f32[48,384]{1,0:T(8,128)}, u32[]{:S(2)}) copy-start(f32[48,384]{1,0:T(8,128)} %param.8) | copy-start | bytes 221188
  51.9 74.3 %collective-permute-start.7 = (bf16[88,32,128]{2,1,0:T(8,128)(2,1)}, bf16[88,32,128]{2,1,0:T(8,128)(2,1)}, u32[]{:S(2)}, u32[]{:S(2)}) collective-permute-start(bf16[88,32,128]{2,1,0:T(8,128)(2,1)} %get-tuple-element.88), channel_id=1, source_target_pairs={{0,4},{4,0},{8,12},{12,8},{16,20},{20,16},{24,28},{28,24},{1,5},{5... | collective-permute-start | bytes 2162696 | tf_op jit(solution)/shard_map/ppermute | solution.py:429
  53.8 74.0 %collective-permute-start.12 = (bf16[88,32,128]{2,1,0:T(8,128)(2,1)}, bf16[88,32,128]{2,1,0:T(8,128)(2,1)}, u32[]{:S(2)}, u32[]{:S(2)}) collective-permute-start(bf16[88,32,128]{2,1,0:T(8,128)(2,1)} %get-tuple-element.86), channel_id=1, source_target_pairs={{0,8},{4,12},{8,0},{12,4},{16,24},{20,28},{24,16},{28,20},{1,9},{5... | collective-permute-start | bytes 2162696 | tf_op jit(solution)/shard_map/ppermute | solution.py:429
  70.4 34.4 %copy-start = (bf16[384,1440]{1,0:T(8,128)(2,1)S(1)}, bf16[384,1440]{1,0:T(8,128)(2,1)}, u32[]{:S(2)}) copy-start(bf16[384,1440]{1,0:T(8,128)(2,1)} %shard_map.76) | copy-start | bytes 3317764
  90.4 43.2 %collective-permute-start.13 = (bf16[88,32,128]{2,1,0:T(8,128)(2,1)}, bf16[88,32,128]{2,1,0:T(8,128)(2,1)}, u32[]{:S(2)}, u32[]{:S(2)}) collective-permute-start(bf16[88,32,128]{2,1,0:T(8,128)(2,1)} %get-tuple-element.85), channel_id=1, source_target_pairs={{0,12},{4,8},{8,4},{12,0},{16,28},{20,24},{24,20},{28,16},{1,13},{... | collective-permute-start | bytes 2162696 | tf_op jit(solution)/shard_map/ppermute | solution.py:429
  100.3 150.1 %collective-permute-start.18 = (bf16[8,400,256]{2,1,0:T(8,128)(2,1)}, bf16[8,400,256]{2,1,0:T(8,128)(2,1)}, u32[]{:S(2)}, u32[]{:S(2)}) collective-permute-start(bf16[8,400,256]{2,1,0:T(8,128)(2,1)} %shard_map.80), channel_id=1, source_target_pairs={{0,16},{4,20},{8,24},{12,28},{16,0},{20,4},{24,8},{28,12},{1,17},{... | collective-permute-start | bytes 4915208 | tf_op jit(solution)/shard_map/ppermute | solution.py:452
  103.3 41.7 %collective-permute-start.3 = (bf16[88,32,128]{2,1,0:T(8,128)(2,1)}, bf16[88,32,128]{2,1,0:T(8,128)(2,1)}, u32[]{:S(2)}, u32[]{:S(2)}) collective-permute-start(bf16[88,32,128]{2,1,0:T(8,128)(2,1)} %get-tuple-element.34), channel_id=1, source_target_pairs={{0,4},{4,0},{8,12},{12,8},{16,20},{20,16},{24,28},{28,24},{1,5},{5... | collective-permute-start | bytes 2162696 | tf_op jit(solution)/shard_map/ppermute | solution.py:429
  126.2 48.7 %collective-permute-start.4 = (bf16[88,32,128]{2,1,0:T(8,128)(2,1)}, bf16[88,32,128]{2,1,0:T(8,128)(2,1)}, u32[]{:S(2)}, u32[]{:S(2)}) collective-permute-start(bf16[88,32,128]{2,1,0:T(8,128)(2,1)} %get-tuple-element.35), channel_id=1, source_target_pairs={{0,8},{4,12},{8,0},{12,4},{16,24},{20,28},{24,16},{28,20},{1,9},{5... | collective-permute-start | bytes 2162696 | tf_op jit(solution)/shard_map/ppermute | solution.py:429
  127.8 64.1 %collective-permute-start.5 = (bf16[88,32,128]{2,1,0:T(8,128)(2,1)S(1)}, bf16[88,32,128]{2,1,0:T(8,128)(2,1)}, u32[]{:S(2)}, u32[]{:S(2)}) collective-permute-start(bf16[88,32,128]{2,1,0:T(8,128)(2,1)S(1)} %get-tuple-element.36), channel_id=1, source_target_pairs={{0,12},{4,8},{8,4},{12,0},{16,28},{20,24},{24,20},{28,16},{1,13},{... | collective-permute-start | bytes 2162696 | tf_op jit(solution)/shard_map/ppermute | solution.py:429
  133.6 68.2 %collective-permute-start.8 = (bf16[88,32,128]{2,1,0:T(8,128)(2,1)S(1)}, bf16[88,32,128]{2,1,0:T(8,128)(2,1)}, u32[]{:S(2)}, u32[]{:S(2)}) collective-permute-start(bf16[88,32,128]{2,1,0:T(8,128)(2,1)S(1)} %get-tuple-element.37), channel_id=1, source_target_pairs={{0,4},{4,0},{8,12},{12,8},{16,20},{20,16},{24,28},{28,24},{1,5},{5... | collective-permute-start | bytes 2162696 | tf_op jit(solution)/shard_map/ppermute | solution.py:429
  145.0 177.1 %collective-permute-start.14 = (bf16[8,400,256]{2,1,0:T(8,128)(2,1)}, bf16[8,400,256]{2,1,0:T(8,128)(2,1)}, u32[]{:S(2)}, u32[]{:S(2)}) collective-permute-start(bf16[8,400,256]{2,1,0:T(8,128)(2,1)} %shard_map.83), channel_id=1, source_target_pairs={{0,16},{4,20},{8,24},{12,28},{16,0},{20,4},{24,8},{28,12},{1,17},{... | collective-permute-start | bytes 4915208 | tf_op jit(solution)/shard_map/ppermute | solution.py:452
  174.9 49.6 %collective-permute-start.19 = (bf16[88,32,128]{2,1,0:T(8,128)(2,1)S(1)}, bf16[88,32,128]{2,1,0:T(8,128)(2,1)}, u32[]{:S(2)}, u32[]{:S(2)}) collective-permute-start(bf16[88,32,128]{2,1,0:T(8,128)(2,1)S(1)} %get-tuple-element.47), channel_id=1, source_target_pairs={{0,8},{4,12},{8,0},{12,4},{16,24},{20,28},{24,16},{28,20},{1,9},{5... | collective-permute-start | bytes 2162696 | tf_op jit(solution)/shard_map/ppermute | solution.py:429
  191.9 58.3 %collective-permute-start.20 = (bf16[88,32,128]{2,1,0:T(8,128)(2,1)S(1)}, bf16[88,32,128]{2,1,0:T(8,128)(2,1)S(1)}, u32[]{:S(2)}, u32[]{:S(2)}) collective-permute-start(bf16[88,32,128]{2,1,0:T(8,128)(2,1)S(1)} %get-tuple-element.48), channel_id=1, source_target_pairs={{0,12},{4,8},{8,4},{12,0},{16,28},{20,24},{24,20},{28,16},{1,13},{... | collective-permute-start | bytes 2162696 | tf_op jit(solution)/shard_map/ppermute | solution.py:429
  201.8 147.4 %collective-permute-start.6 = (bf16[8,400,256]{2,1,0:T(8,128)(2,1)}, bf16[8,400,256]{2,1,0:T(8,128)(2,1)}, u32[]{:S(2)}, u32[]{:S(2)}) collective-permute-start(bf16[8,400,256]{2,1,0:T(8,128)(2,1)} %shard_map.82), channel_id=1, source_target_pairs={{0,16},{4,20},{8,24},{12,28},{16,0},{20,4},{24,8},{28,12},{1,17},{... | collective-permute-start | bytes 4915208 | tf_op jit(solution)/shard_map/ppermute | solution.py:452
  224.5 55.6 %collective-permute-start.15 = (bf16[88,32,128]{2,1,0:T(8,128)(2,1)S(1)}, bf16[88,32,128]{2,1,0:T(8,128)(2,1)S(1)}, u32[]{:S(2)}, u32[]{:S(2)}) collective-permute-start(bf16[88,32,128]{2,1,0:T(8,128)(2,1)S(1)} %get-tuple-element.43), channel_id=1, source_target_pairs={{0,4},{4,0},{8,12},{12,8},{16,20},{20,16},{24,28},{28,24},{1,5},{5... | collective-permute-start | bytes 2162696 | tf_op jit(solution)/shard_map/ppermute | solution.py:429
  250.2 3.6 copy-start.3
  250.2 39.8 %collective-permute-start.16 = (bf16[88,32,128]{2,1,0:T(8,128)(2,1)S(1)}, bf16[88,32,128]{2,1,0:T(8,128)(2,1)S(1)}, u32[]{:S(2)}, u32[]{:S(2)}) collective-permute-start(bf16[88,32,128]{2,1,0:T(8,128)(2,1)S(1)} %get-tuple-element.44), channel_id=1, source_target_pairs={{0,8},{4,12},{8,0},{12,4},{16,24},{20,28},{24,16},{28,20},{1,9},{5... | collective-permute-start | bytes 2162696 | tf_op jit(solution)/shard_map/ppermute | solution.py:429
  250.4 71.6 %collective-permute-start.17 = (bf16[88,32,128]{2,1,0:T(8,128)(2,1)S(1)}, bf16[88,32,128]{2,1,0:T(8,128)(2,1)S(1)}, u32[]{:S(2)}, u32[]{:S(2)}) collective-permute-start(bf16[88,32,128]{2,1,0:T(8,128)(2,1)S(1)} %get-tuple-element.45), channel_id=1, source_target_pairs={{0,12},{4,8},{8,4},{12,0},{16,28},{20,24},{24,20},{28,16},{1,13},{... | collective-permute-start | bytes 2162696 | tf_op jit(solution)/shard_map/ppermute | solution.py:429
  280.2 41.9 %copy-start.4 = (bf16[88,32,128]{2,1,0:T(8,128)(2,1)}, bf16[88,32,128]{2,1,0:T(8,128)(2,1)S(1)}, u32[]{:S(2)}) copy-start(bf16[88,32,128]{2,1,0:T(8,128)(2,1)S(1)} %collective-permute-done.15.rest_1_) | copy-start | bytes 2162692
  280.2 68.9 %collective-permute-start.9 = (bf16[88,32,128]{2,1,0:T(8,128)(2,1)S(1)}, bf16[88,32,128]{2,1,0:T(8,128)(2,1)S(1)}, u32[]{:S(2)}, u32[]{:S(2)}) collective-permute-start(bf16[88,32,128]{2,1,0:T(8,128)(2,1)S(1)} %get-tuple-element.39), channel_id=1, source_target_pairs={{0,4},{4,0},{8,12},{12,8},{16,20},{20,16},{24,28},{28,24},{1,5},{5... | collective-permute-start | bytes 2162696 | tf_op jit(solution)/shard_map/ppermute | solution.py:429
  290.0 32.1 %copy-start.6 = (bf16[88,32,128]{2,1,0:T(8,128)(2,1)}, bf16[88,32,128]{2,1,0:T(8,128)(2,1)S(1)}, u32[]{:S(2)}) copy-start(bf16[88,32,128]{2,1,0:T(8,128)(2,1)S(1)} %collective-permute-done.16.rest_2_) | copy-start | bytes 2162692
  290.0 59.1 %collective-permute-start.10 = (bf16[88,32,128]{2,1,0:T(8,128)(2,1)S(1)}, bf16[88,32,128]{2,1,0:T(8,128)(2,1)S(1)}, u32[]{:S(2)}, u32[]{:S(2)}) collective-permute-start(bf16[88,32,128]{2,1,0:T(8,128)(2,1)S(1)} %get-tuple-element.40), channel_id=1, source_target_pairs={{0,8},{4,12},{8,0},{12,4},{16,24},{20,28},{24,16},{28,20},{1,9},{5... | collective-permute-start | bytes 2162696 | tf_op jit(solution)/shard_map/ppermute | solution.py:429
  322.1 0.9 copy-start.8
  322.1 27.1 %collective-permute-start.11 = (bf16[88,32,128]{2,1,0:T(8,128)(2,1)S(1)}, bf16[88,32,128]{2,1,0:T(8,128)(2,1)S(1)}, u32[]{:S(2)}, u32[]{:S(2)}) collective-permute-start(bf16[88,32,128]{2,1,0:T(8,128)(2,1)S(1)} %get-tuple-element.41), channel_id=1, source_target_pairs={{0,12},{4,8},{8,4},{12,0},{16,28},{20,24},{24,20},{28,16},{1,13},{... | collective-permute-start | bytes 2162696 | tf_op jit(solution)/shard_map/ppermute | solution.py:429
  349.1 0.9 copy-start.5
  349.1 1.1 copy-start.7
  349.2 1.3 copy-start.9
  376.7 5.8 %collective-permute-start.21 = (bf16[2,48,384]{2,0,1:T(2,128)(2,1)S(1)}, bf16[2,48,384]{2,0,1:T(2,128)(2,1)S(1)}, u32[]{:S(2)}, u32[]{:S(2)}) collective-permute-start(bf16[2,48,384]{2,0,1:T(2,128)(2,1)S(1)} %slice.340), channel_id=1, source_target_pairs={{0,1},{1,2},{2,3},{4,5},{5,6},{6,7},{8,9},{9,10},{10,11},{12,13},{... | collective-permute-start | bytes 221192 | tf_op jit(solution)/shard_map/ppermute | solution.py:491
  379.0 9.9 %all-to-all-start = ((bf16[4,48,6,96]{3,1,2,0:T(8,128)(2,1)}), bf16[4,48,6,96]{3,1,2,0:T(8,128)(2,1)S(1)}, u32[]{:S(2)}, u32[]{:S(2)}) async-start(bf16[4,48,6,96]{3,1,2,0:T(8,128)(2,1)} %copy.113), calls=%async_computation | async-start | bytes 589824 | tf_op jit(solution)/shard_map/all_to_all | solution.py:499
